TPU v7x, 32 devices: a whole 2x2x4 slice. The times are simulated.
32 devices in a mesh: dp: 8 (over z, x), ctx: 2 (over core), tp: 2 (over y).
Axes of the slice: x: 2, y: 2, z: 4, core: 2. Of those that a mesh axis runs over, the one named last changes fastest.
Arguments:
- hidden_in: bfloat16 [16, 1024, 1024], P('dp', 'ctx'), may hold values from -6 to 6
- cotangent: bfloat16 [16, 1024, 1024], P('dp', 'ctx'), may hold values from -6 to 6
- attn_norm_gain: float32 [1024], replicated, may hold values from 0.5 to 1.5
- ffn_norm_gain: float32 [1024], replicated, may hold values from 0.5 to 1.5
- w_query: bfloat16 [1024, 512], P(('dp', 'ctx'), 'tp'), may hold values from -0.1875 to 0.1875
- key_weight: bfloat16 [1024, 128], P(('dp', 'ctx'), 'tp'), may hold values from -0.1875 to 0.1875
- value_weight: bfloat16 [1024, 128], P(('dp', 'ctx'), 'tp'), may hold values from -0.1875 to 0.1875
- w_attn_out: bfloat16 [512, 1024], P('tp', ('dp', 'ctx')), may hold values from -2 to 2
- mixer_input_weight: bfloat16 [1024, 1536], P(('dp', 'ctx'), 'tp'), may hold values from -0.1875 to 0.1875
- mixer_gate_weight: bfloat16 [1024, 1536], P(('dp', 'ctx'), 'tp'), may hold values from -0.1875 to 0.1875
- w_ssm_bc: bfloat16 [1024, 256], P(('dp', 'ctx')), may hold values from -0.1875 to 0.1875
- w_ssm_dt: bfloat16 [1024, 24], P(('dp', 'ctx'), 'tp'), may hold values from -0.1875 to 0.1875
- dt_bias: float32 [24], P('tp'), may hold values from -4 to -1
- a_log: float32 [24], P('tp'), may hold values from -2 to 1.5
- d_skip: float32 [24], P('tp'), may hold values from 0.5 to 1.5
- input_conv_taps: float32 [4, 1536], P(None, 'tp'), may hold values from -3 to 3
- conv_bc: float32 [4, 256], replicated, may hold values from -3 to 3
- mixer_output_weight: bfloat16 [1536, 1024], P('tp', ('dp', 'ctx')), may hold values from -0.4375 to 0.4375
- w_gate: bfloat16 [1024, 2048], P(('dp', 'ctx'), 'tp'), may hold values from -0.1875 to 0.1875
- w_up: bfloat16 [1024, 2048], P(('dp', 'ctx'), 'tp'), may hold values from -0.1875 to 0.1875
- w_down: bfloat16 [2048, 1024], P('tp', ('dp', 'ctx')), may hold values from -0.25 to 0.25
Outputs:
- out: bfloat16 [16, 1024, 1024], P('dp', 'ctx')
- grad_in: bfloat16 [16, 1024, 1024], P('dp', 'ctx')
- grad_attn_norm_gain: float32 [1024], replicated
- grad_ffn_norm_gain: float32 [1024], replicated
- grad_w_query: float32 [1024, 512], P(('dp', 'ctx'), 'tp')
- grad_w_key: float32 [1024, 128], P(('dp', 'ctx'), 'tp')
- grad_w_value: float32 [1024, 128], P(('dp', 'ctx'), 'tp')
- grad_w_attn_out: float32 [512, 1024], P('tp', ('dp', 'ctx'))
- grad_w_ssm_x: float32 [1024, 1536], P(('dp', 'ctx'), 'tp')
- grad_w_ssm_gate: float32 [1024, 1536], P(('dp', 'ctx'), 'tp')
- grad_w_ssm_bc: float32 [1024, 256], P(('dp', 'ctx'))
- grad_w_ssm_dt: float32 [1024, 24], P(('dp', 'ctx'), 'tp')
- grad_dt_bias: float32 [24], P('tp')
- grad_a_log: float32 [24], P('tp')
- grad_d_skip: float32 [24], P('tp')
- grad_conv_x: float32 [4, 1536], P(None, 'tp')
- grad_conv_bc: float32 [4, 256], replicated
- grad_w_ssm_out: float32 [1536, 1024], P('tp', ('dp', 'ctx'))
- grad_w_gate: float32 [1024, 2048], P(('dp', 'ctx'), 'tp')
- grad_w_up: float32 [1024, 2048], P(('dp', 'ctx'), 'tp')
- grad_w_down: float32 [2048, 1024], P('tp', ('dp', 'ctx'))
All inputs are finite; a program needn't handle non-finite values.
Results may differ from a plain program's by a relative error of at most 0.018.
Values may be sent and summed in bfloat16 or wider, within the bound.
A program may use at most 192 MiB of HBM per device.

v0:
```python
import jax
import jax.numpy as jnp
from jax import lax
from jax.sharding import PartitionSpec as P

QUERY_HEADS = 8
KEY_VALUE_HEADS = 2
ATTN_HEAD_SIZE = 64
MIXER_HEAD_SIZE = 64
NS = 128
CONV_TAPS = 4
SPAN = 256


TOP_PRECISION = lax.Precision.HIGHEST
EPSILON = 1e-05
ROPE_BASE = 10000.0


def rms_scale(values, gain_row):
    return (
        values * lax.rsqrt(jnp.mean(values * values, axis=-1, keepdims=True) + EPSILON) * gain_row
    )


def rope_turn(values):
    half_dim = values.shape[-1] // 2
    position = jnp.arange(values.shape[0], dtype=jnp.float32)
    frequency = ROPE_BASE ** (-jnp.arange(half_dim, dtype=jnp.float32) / half_dim)
    angles = position[:, None] * frequency[None, :]
    cosine = jnp.cos(angles)[:, None, :]
    sine_part = jnp.sin(angles)[:, None, :]
    first_half = values[..., :half_dim]
    second_half = values[..., half_dim:]
    return jnp.concatenate(
        [
            first_half * cosine - second_half * sine_part,
            second_half * cosine + first_half * sine_part,
        ],
        axis=-1,
    )


def attend_one(queries, key_rows, value_rows):
    length = queries.shape[0]
    turned_queries = rope_turn(queries).astype(jnp.bfloat16)
    turned_keys = rope_turn(key_rows).astype(jnp.bfloat16)
    scores = jnp.einsum(
        "qhd,khd->hqk", turned_queries, turned_keys, preferred_element_type=jnp.float32
    ) * queries.shape[-1] ** (-0.5)
    positions = jnp.arange(length)
    causal = positions[None, :] <= positions[:, None]
    scores = jnp.where(causal[None, :, :], scores, -1e30)
    weights = jax.nn.softmax(scores, axis=-1).astype(jnp.bfloat16)
    return jnp.einsum(
        "hqk,khd->qhd", weights, value_rows.astype(jnp.bfloat16), preferred_element_type=jnp.float32
    )


def block_step(carry_state, pieces):
    ssm_heads, write_rows, read_rows, step_size, log_decay = pieces
    cumulative = jnp.cumsum(log_decay, axis=0)
    block_rows = cumulative.shape[0]
    log_gap = cumulative[:, None, :] - cumulative[None, :, :]
    positions = jnp.arange(block_rows)
    lower_mask = (positions[None, :] <= positions[:, None])[:, :, None]
    decay_table = jnp.exp(jnp.where(lower_mask, log_gap, -1e30))
    pairing = jnp.einsum("tn,sn->ts", read_rows, write_rows, precision=TOP_PRECISION)
    mixing = pairing[:, :, None] * decay_table * step_size[None, :, :]
    within = jnp.einsum("tsh,shp->thp", mixing, ssm_heads, precision=TOP_PRECISION)
    carried = (
        jnp.einsum("tn,hpn->thp", read_rows, carry_state, precision=TOP_PRECISION)
        * jnp.exp(cumulative)[:, :, None]
    )
    last_row = cumulative[block_rows - 1]
    tail_weight = jnp.exp(last_row[None, :] - cumulative) * step_size
    new_state = jnp.exp(last_row)[:, None, None] * carry_state + jnp.einsum(
        "sh,shp,sn->hpn", tail_weight, ssm_heads, write_rows, precision=TOP_PRECISION
    )
    return (new_state, within + carried)


def ssd_one(mixer_input, shared_in, dt_raw, dt_shift, log_rate, skip_gain, conv_ssm, conv_common):
    length = mixer_input.shape[0]
    head_count = dt_raw.shape[-1]
    head_dim = mixer_input.shape[-1] // head_count
    state_dim = shared_in.shape[-1] // 2
    joined = jnp.concatenate([mixer_input, shared_in], axis=-1)
    kernel = jnp.concatenate([conv_ssm, conv_common], axis=-1)
    tap_count = kernel.shape[0]
    padded = jnp.pad(joined, ((tap_count - 1, 0), (0, 0)))
    convolved = kernel[0] * padded[0:length]
    for offset in range(1, tap_count):
        convolved = convolved + kernel[offset] * padded[offset : offset + length]
    active = jax.nn.silu(convolved)
    split_at = head_count * head_dim
    ssm_heads = active[:, :split_at].reshape(length, head_count, head_dim)
    write_rows = active[:, split_at : split_at + state_dim]
    read_rows = active[:, split_at + state_dim :]
    step_size = jax.nn.softplus(dt_raw + dt_shift)
    log_decay = -step_size * jnp.exp(log_rate)
    blocks = length // SPAN
    pieces = (
        ssm_heads.reshape(blocks, SPAN, head_count, head_dim),
        write_rows.reshape(blocks, SPAN, state_dim),
        read_rows.reshape(blocks, SPAN, state_dim),
        step_size.reshape(blocks, SPAN, head_count),
        log_decay.reshape(blocks, SPAN, head_count),
    )
    start_state = jnp.zeros((head_count, head_dim, state_dim), jnp.float32)
    final_state, outputs = lax.scan(jax.checkpoint(block_step), start_state, pieces)
    result = outputs.reshape(length, head_count, head_dim) + skip_gain[None, :, None] * ssm_heads
    return result.reshape(length, head_count * head_dim)


def plain_dot(operand, weight_matrix):
    return jnp.dot(operand, weight_matrix, preferred_element_type=jnp.float32)


def dot_back(operand, weight_matrix):
    return lax.dot_general(
        operand, weight_matrix, (((1,), (1,)), ((), ())), preferred_element_type=jnp.float32
    )


def dot_left(operand, weight_matrix):
    return lax.dot_general(
        operand, weight_matrix, (((0,), (0,)), ((), ())), preferred_element_type=jnp.float32
    )


def gate_silu(gate_in, other_rows):
    return jax.nn.silu(gate_in) * other_rows


def per_device(
    hidden_in,
    cotangent,
    attn_norm_gain,
    ffn_norm_gain,
    w_query,
    key_weight,
    value_weight,
    w_attn_out,
    mixer_input_weight,
    mixer_gate_weight,
    w_ssm_bc,
    w_ssm_dt,
    dt_bias,
    a_log,
    d_skip,
    input_conv_taps,
    conv_bc,
    mixer_output_weight,
    w_gate,
    w_up,
    w_down,
):
    sequence_count, halved_length, model_width = hidden_in.shape
    count_of_rows = sequence_count * halved_length
    ctx_size = lax.axis_size("ctx")
    context_positions = lax.axis_index("ctx")
    complete_length = halved_length * ctx_size
    local_query = w_query.shape[1] // ATTN_HEAD_SIZE
    local_kv = key_weight.shape[1] // ATTN_HEAD_SIZE
    local_mixer = w_ssm_dt.shape[1]
    query_part = local_query // ctx_size
    mixer_portion = local_mixer // ctx_size
    sharing_count = QUERY_HEADS // KEY_VALUE_HEADS
    (
        full_query,
        full_key,
        full_value,
        full_ssm_x,
        full_ssm_gate,
        full_shared,
        full_dt,
        full_gate,
        full_up,
        full_attn_out,
        full_ssm_out,
        full_down,
    ) = (
        lax.all_gather(w_query, ("dp", "ctx"), axis=0, tiled=True),
        lax.all_gather(key_weight, ("dp", "ctx"), axis=0, tiled=True),
        lax.all_gather(value_weight, ("dp", "ctx"), axis=0, tiled=True),
        lax.all_gather(mixer_input_weight, ("dp", "ctx"), axis=0, tiled=True),
        lax.all_gather(mixer_gate_weight, ("dp", "ctx"), axis=0, tiled=True),
        lax.all_gather(w_ssm_bc, ("dp", "ctx"), axis=0, tiled=True),
        lax.all_gather(w_ssm_dt, ("dp", "ctx"), axis=0, tiled=True),
        lax.all_gather(w_gate, ("dp", "ctx"), axis=0, tiled=True),
        lax.all_gather(w_up, ("dp", "ctx"), axis=0, tiled=True),
        lax.all_gather(w_attn_out, ("dp", "ctx"), axis=1, tiled=True),
        lax.all_gather(mixer_output_weight, ("dp", "ctx"), axis=1, tiled=True),
        lax.all_gather(w_down, ("dp", "ctx"), axis=1, tiled=True),
    )
    hidden = hidden_in.astype(jnp.float32).reshape(count_of_rows, model_width)
    normed_full, attn_norm_pull = jax.vjp(rms_scale, hidden, attn_norm_gain)
    normed = normed_full.astype(jnp.bfloat16)
    queries = plain_dot(normed, full_query).astype(jnp.bfloat16)
    key_rows = plain_dot(normed, full_key).astype(jnp.bfloat16)
    value_rows = plain_dot(normed, full_value).astype(jnp.bfloat16)
    mixer_input = plain_dot(normed, full_ssm_x).astype(jnp.bfloat16)
    shared_rows = plain_dot(normed, full_shared).astype(jnp.bfloat16)
    dt_raw = plain_dot(normed, full_dt).astype(jnp.bfloat16)
    gate_ssm = plain_dot(normed, full_ssm_gate)
    head_query, mixer_head_rows, head_dt = (
        lax.all_to_all(
            queries.reshape(sequence_count, halved_length, local_query, ATTN_HEAD_SIZE),
            "ctx",
            split_axis=2,
            concat_axis=1,
            tiled=True,
        ),
        lax.all_to_all(
            mixer_input.reshape(sequence_count, halved_length, local_mixer, MIXER_HEAD_SIZE),
            "ctx",
            split_axis=2,
            concat_axis=1,
            tiled=True,
        ),
        lax.all_to_all(
            dt_raw.reshape(sequence_count, halved_length, local_mixer, 1),
            "ctx",
            split_axis=2,
            concat_axis=1,
            tiled=True,
        ),
    )
    seq_keys, seq_values, seq_shared = (
        lax.all_gather(
            key_rows.reshape(sequence_count, halved_length, local_kv * ATTN_HEAD_SIZE),
            "ctx",
            axis=1,
            tiled=True,
        ),
        lax.all_gather(
            value_rows.reshape(sequence_count, halved_length, local_kv * ATTN_HEAD_SIZE),
            "ctx",
            axis=1,
            tiled=True,
        ),
        lax.all_gather(
            shared_rows.reshape(sequence_count, halved_length, 2 * NS), "ctx", axis=1, tiled=True
        ),
    )
    head_ids = (context_positions * query_part + jnp.arange(query_part)) // sharing_count
    shift_local = lax.dynamic_slice_in_dim(
        dt_bias, context_positions * mixer_portion, mixer_portion
    )
    rate_local = lax.dynamic_slice_in_dim(a_log, context_positions * mixer_portion, mixer_portion)
    skip_local = lax.dynamic_slice_in_dim(d_skip, context_positions * mixer_portion, mixer_portion)
    local_convolution = lax.dynamic_slice_in_dim(
        input_conv_taps,
        context_positions * mixer_portion * MIXER_HEAD_SIZE,
        mixer_portion * MIXER_HEAD_SIZE,
        1,
    )

    def mixer(
        query_in,
        key_in,
        value_in,
        ssm_seq,
        shared_seq,
        dt_seq,
        dt_shift,
        log_rate,
        skip_gain,
        conv_ssm,
        conv_common,
    ):

        def attend_seq(pieces):
            query_one, single_key, single_value = pieces
            broadened_keys = jnp.take(
                single_key.reshape(complete_length, local_kv, ATTN_HEAD_SIZE), head_ids, axis=1
            )
            broadened_values = jnp.take(
                single_value.reshape(complete_length, local_kv, ATTN_HEAD_SIZE), head_ids, axis=1
            )
            return attend_one(query_one, broadened_keys, broadened_values)

        def ssd_seq(pieces):
            ssm_one, shared_one, dt_one = pieces
            return ssd_one(
                ssm_one, shared_one, dt_one, dt_shift, log_rate, skip_gain, conv_ssm, conv_common
            )

        attended = lax.map(jax.checkpoint(attend_seq), (query_in, key_in, value_in))
        scan_result = lax.map(jax.checkpoint(ssd_seq), (ssm_seq, shared_seq, dt_seq))
        return (attended, scan_result)

    (attended, scan_result), mixer_pull = jax.vjp(
        mixer,
        head_query.astype(jnp.float32),
        seq_keys.astype(jnp.float32),
        seq_values.astype(jnp.float32),
        mixer_head_rows.astype(jnp.float32).reshape(
            sequence_count, complete_length, mixer_portion * MIXER_HEAD_SIZE
        ),
        seq_shared.astype(jnp.float32),
        head_dt.astype(jnp.float32).reshape(sequence_count, complete_length, mixer_portion),
        shift_local,
        rate_local,
        skip_local,
        local_convolution,
        conv_bc,
    )
    row_attn, mixer_per_row = (
        lax.all_to_all(
            attended.astype(jnp.bfloat16), "ctx", split_axis=1, concat_axis=2, tiled=True
        ),
        lax.all_to_all(
            scan_result.astype(jnp.bfloat16).reshape(
                sequence_count, complete_length, mixer_portion, MIXER_HEAD_SIZE
            ),
            "ctx",
            split_axis=1,
            concat_axis=2,
            tiled=True,
        ),
    )
    attn_rows = row_attn.reshape(count_of_rows, local_query * ATTN_HEAD_SIZE)
    mixer_rows = mixer_per_row.reshape(count_of_rows, local_mixer * MIXER_HEAD_SIZE)
    gated_full, gate_pull = jax.vjp(gate_silu, gate_ssm, mixer_rows.astype(jnp.float32))
    gated_rows = gated_full.astype(jnp.bfloat16)
    mixed_sum = lax.psum(
        (plain_dot(attn_rows, full_attn_out) + plain_dot(gated_rows, full_ssm_out)).astype(
            jnp.bfloat16
        ),
        "tp",
    ).astype(jnp.float32)
    middle = hidden + mixed_sum
    normed_ffn_full, ffn_norm_pull = jax.vjp(rms_scale, middle, ffn_norm_gain)
    normed_ffn = normed_ffn_full.astype(jnp.bfloat16)
    gate_rows = plain_dot(normed_ffn, full_gate)
    up_rows = plain_dot(normed_ffn, full_up)
    inner_full, inner_pull = jax.vjp(gate_silu, gate_rows, up_rows)
    inner_rows = inner_full.astype(jnp.bfloat16)
    ffn_out = lax.psum(plain_dot(inner_rows, full_down).astype(jnp.bfloat16), "tp").astype(
        jnp.float32
    )
    output = (
        (middle + ffn_out).astype(jnp.bfloat16).reshape(sequence_count, halved_length, model_width)
    )
    (
        full_query,
        full_key,
        full_value,
        full_ssm_x,
        full_ssm_gate,
        full_shared,
        full_dt,
        full_gate,
        full_up,
        full_attn_out,
        full_ssm_out,
        full_down,
    ) = (
        lax.all_gather(w_query, ("dp", "ctx"), axis=0, tiled=True),
        lax.all_gather(key_weight, ("dp", "ctx"), axis=0, tiled=True),
        lax.all_gather(value_weight, ("dp", "ctx"), axis=0, tiled=True),
        lax.all_gather(mixer_input_weight, ("dp", "ctx"), axis=0, tiled=True),
        lax.all_gather(mixer_gate_weight, ("dp", "ctx"), axis=0, tiled=True),
        lax.all_gather(w_ssm_bc, ("dp", "ctx"), axis=0, tiled=True),
        lax.all_gather(w_ssm_dt, ("dp", "ctx"), axis=0, tiled=True),
        lax.all_gather(w_gate, ("dp", "ctx"), axis=0, tiled=True),
        lax.all_gather(w_up, ("dp", "ctx"), axis=0, tiled=True),
        lax.all_gather(w_attn_out, ("dp", "ctx"), axis=1, tiled=True),
        lax.all_gather(mixer_output_weight, ("dp", "ctx"), axis=1, tiled=True),
        lax.all_gather(w_down, ("dp", "ctx"), axis=1, tiled=True),
    )
    grad_rows = cotangent.reshape(count_of_rows, model_width)
    grad_inner = dot_back(grad_rows, full_down)
    grad_w_down = dot_left(inner_rows, grad_rows)
    grad_gate_full, grad_up_full = inner_pull(grad_inner)
    grad_gate = grad_gate_full.astype(jnp.bfloat16)
    grad_up = grad_up_full.astype(jnp.bfloat16)
    grad_w_gate = dot_left(normed_ffn, grad_gate)
    grad_w_up = dot_left(normed_ffn, grad_up)
    grad_ffn_in = lax.psum(dot_back(grad_gate, full_gate) + dot_back(grad_up, full_up), "tp")
    grad_middle_norm, grad_ffn_gain = ffn_norm_pull(grad_ffn_in)
    grad_middle = (
        cotangent.astype(jnp.float32).reshape(count_of_rows, model_width) + grad_middle_norm
    )
    grad_mixed = grad_middle.astype(jnp.bfloat16)
    grad_w_attn_out = dot_left(attn_rows, grad_mixed)
    grad_w_ssm_out = dot_left(gated_rows, grad_mixed)
    grad_attn_rows = dot_back(grad_mixed, full_attn_out).astype(jnp.bfloat16)
    grad_gated = dot_back(grad_mixed, full_ssm_out)
    grad_gate_ssm_full, mixer_row_gradient = gate_pull(grad_gated)
    grad_gate_ssm = grad_gate_ssm_full.astype(jnp.bfloat16)
    head_grad_attn, gradient_mixer_heads = (
        lax.all_to_all(
            grad_attn_rows.reshape(sequence_count, halved_length, local_query, ATTN_HEAD_SIZE),
            "ctx",
            split_axis=2,
            concat_axis=1,
            tiled=True,
        ),
        lax.all_to_all(
            mixer_row_gradient.astype(jnp.bfloat16).reshape(
                sequence_count, halved_length, local_mixer, MIXER_HEAD_SIZE
            ),
            "ctx",
            split_axis=2,
            concat_axis=1,
            tiled=True,
        ),
    )
    (
        grad_head_query,
        grad_seq_keys,
        grad_seq_values,
        mixer_head_gradient,
        grad_seq_shared,
        grad_head_dt,
        grad_shift,
        grad_rate,
        grad_skip,
        grad_conv_ssm,
        grad_conv_common,
    ) = mixer_pull(
        (
            head_grad_attn.astype(jnp.float32),
            gradient_mixer_heads.astype(jnp.float32).reshape(
                sequence_count, complete_length, mixer_portion * MIXER_HEAD_SIZE
            ),
        )
    )
    back_query, mixer_backward, back_dt = (
        lax.all_to_all(
            grad_head_query.astype(jnp.bfloat16), "ctx", split_axis=1, concat_axis=2, tiled=True
        ),
        lax.all_to_all(
            mixer_head_gradient.astype(jnp.bfloat16).reshape(
                sequence_count, complete_length, mixer_portion, MIXER_HEAD_SIZE
            ),
            "ctx",
            split_axis=1,
            concat_axis=2,
            tiled=True,
        ),
        lax.all_to_all(
            grad_head_dt.astype(jnp.bfloat16).reshape(
                sequence_count, complete_length, mixer_portion, 1
            ),
            "ctx",
            split_axis=1,
            concat_axis=2,
            tiled=True,
        ),
    )
    back_keys, back_values, back_shared = (
        lax.psum_scatter(
            grad_seq_keys.astype(jnp.bfloat16), "ctx", scatter_dimension=1, tiled=True
        ).astype(jnp.float32),
        lax.psum_scatter(
            grad_seq_values.astype(jnp.bfloat16), "ctx", scatter_dimension=1, tiled=True
        ).astype(jnp.float32),
        lax.psum_scatter(
            grad_seq_shared.astype(jnp.bfloat16), "ctx", scatter_dimension=1, tiled=True
        ).astype(jnp.float32),
    )
    grad_query_rows = back_query.reshape(count_of_rows, local_query * ATTN_HEAD_SIZE)
    mixer_input_gradient = mixer_backward.reshape(count_of_rows, local_mixer * MIXER_HEAD_SIZE)
    grad_dt_rows = back_dt.reshape(count_of_rows, local_mixer)
    grad_key_rows = back_keys.reshape(count_of_rows, local_kv * ATTN_HEAD_SIZE).astype(jnp.bfloat16)
    grad_value_rows = back_values.reshape(count_of_rows, local_kv * ATTN_HEAD_SIZE).astype(
        jnp.bfloat16
    )
    partial_in = (
        dot_back(grad_query_rows, full_query)
        + dot_back(grad_key_rows, full_key)
        + dot_back(grad_value_rows, full_value)
        + dot_back(mixer_input_gradient, full_ssm_x)
        + dot_back(grad_gate_ssm, full_ssm_gate)
        + dot_back(grad_dt_rows, full_dt)
    )
    summed_in, summed_shared, summed_conv = (
        lax.psum(partial_in.astype(jnp.bfloat16), "tp").astype(jnp.float32),
        lax.psum(back_shared.reshape(count_of_rows, 2 * NS).astype(jnp.bfloat16), "tp").astype(
            jnp.float32
        ),
        lax.psum(grad_conv_common.astype(jnp.bfloat16), "tp").astype(jnp.float32),
    )
    grad_shared_rows = summed_shared.astype(jnp.bfloat16)
    grad_normed = summed_in + dot_back(grad_shared_rows, full_shared)
    grad_hidden_norm, grad_attn_gain = attn_norm_pull(grad_normed)
    grad_input = (
        (grad_middle + grad_hidden_norm)
        .astype(jnp.bfloat16)
        .reshape(sequence_count, halved_length, model_width)
    )
    pad_shift = lax.dynamic_update_slice(
        jnp.zeros((local_mixer,), jnp.float32), grad_shift, (context_positions * mixer_portion,)
    )
    pad_rate = lax.dynamic_update_slice(
        jnp.zeros((local_mixer,), jnp.float32), grad_rate, (context_positions * mixer_portion,)
    )
    pad_skip = lax.dynamic_update_slice(
        jnp.zeros((local_mixer,), jnp.float32), grad_skip, (context_positions * mixer_portion,)
    )
    pad_conv = lax.dynamic_update_slice(
        jnp.zeros((CONV_TAPS, local_mixer * MIXER_HEAD_SIZE), jnp.float32),
        grad_conv_ssm,
        (context_positions * 0, context_positions * mixer_portion * MIXER_HEAD_SIZE),
    )
    small_sums = lax.psum(
        (grad_attn_gain, grad_ffn_gain, pad_shift, pad_rate, pad_skip, pad_conv, summed_conv),
        ("dp", "ctx"),
    )
    weight_grads = (
        lax.psum_scatter(
            dot_left(normed, grad_query_rows), ("dp", "ctx"), scatter_dimension=0, tiled=True
        ),
        lax.psum_scatter(
            dot_left(normed, grad_key_rows), ("dp", "ctx"), scatter_dimension=0, tiled=True
        ),
        lax.psum_scatter(
            dot_left(normed, grad_value_rows), ("dp", "ctx"), scatter_dimension=0, tiled=True
        ),
        lax.psum_scatter(
            dot_left(normed, mixer_input_gradient), ("dp", "ctx"), scatter_dimension=0, tiled=True
        ),
        lax.psum_scatter(
            dot_left(normed, grad_gate_ssm), ("dp", "ctx"), scatter_dimension=0, tiled=True
        ),
        lax.psum_scatter(
            dot_left(normed, grad_shared_rows), ("dp", "ctx"), scatter_dimension=0, tiled=True
        ),
        lax.psum_scatter(
            dot_left(normed, grad_dt_rows), ("dp", "ctx"), scatter_dimension=0, tiled=True
        ),
        lax.psum_scatter(grad_w_gate, ("dp", "ctx"), scatter_dimension=0, tiled=True),
        lax.psum_scatter(grad_w_up, ("dp", "ctx"), scatter_dimension=0, tiled=True),
        lax.psum_scatter(grad_w_attn_out, ("dp", "ctx"), scatter_dimension=1, tiled=True),
        lax.psum_scatter(grad_w_ssm_out, ("dp", "ctx"), scatter_dimension=1, tiled=True),
        lax.psum_scatter(grad_w_down, ("dp", "ctx"), scatter_dimension=1, tiled=True),
    )
    return (
        output,
        grad_input,
        small_sums[0],
        small_sums[1],
        weight_grads[0],
        weight_grads[1],
        weight_grads[2],
        weight_grads[9],
        weight_grads[3],
        weight_grads[4],
        weight_grads[5],
        weight_grads[6],
        small_sums[2],
        small_sums[3],
        small_sums[4],
        small_sums[5],
        small_sums[6],
        weight_grads[10],
        weight_grads[7],
        weight_grads[8],
        weight_grads[11],
    )


def solution(mesh):
    in_specs = (
        P("dp", "ctx", None),
        P("dp", "ctx", None),
        P(),
        P(),
        P(("dp", "ctx"), "tp"),
        P(("dp", "ctx"), "tp"),
        P(("dp", "ctx"), "tp"),
        P("tp", ("dp", "ctx")),
        P(("dp", "ctx"), "tp"),
        P(("dp", "ctx"), "tp"),
        P(("dp", "ctx"), None),
        P(("dp", "ctx"), "tp"),
        P("tp"),
        P("tp"),
        P("tp"),
        P(None, "tp"),
        P(),
        P("tp", ("dp", "ctx")),
        P(("dp", "ctx"), "tp"),
        P(("dp", "ctx"), "tp"),
        P("tp", ("dp", "ctx")),
    )
    out_specs = (
        P("dp", "ctx", None),
        P("dp", "ctx", None),
        P(),
        P(),
        P(("dp", "ctx"), "tp"),
        P(("dp", "ctx"), "tp"),
        P(("dp", "ctx"), "tp"),
        P("tp", ("dp", "ctx")),
        P(("dp", "ctx"), "tp"),
        P(("dp", "ctx"), "tp"),
        P(("dp", "ctx"), None),
        P(("dp", "ctx"), "tp"),
        P("tp"),
        P("tp"),
        P("tp"),
        P(None, "tp"),
        P(),
        P("tp", ("dp", "ctx")),
        P(("dp", "ctx"), "tp"),
        P(("dp", "ctx"), "tp"),
        P("tp", ("dp", "ctx")),
    )
    return jax.shard_map(
        per_device, mesh=mesh, in_specs=in_specs, out_specs=out_specs, check_vma=False
    )
```

profile of v0, /device:TPU:0, one launch (start us, length us, event | category | flops | bytes accessed | tf_op | source)
XLA Modules:
  0.0 2560.6 jit_solution(6361560230378219262)
XLA Ops:
  10.7 24.8 all_gather.65
  39.9 18.9 all_gather.59
  70.6 19.9 all-gather
  90.6 18.1 all_gather.60
  108.7 20.1 all_gather.57
  128.8 21.2 all_gather.62
  167.1 34.0 %while.196 = (s32[]{:T(128)}, bf16[2,1024,2,64]{1,3,2,0:T(8,128)(2,1)}, bf16[2,1024,64]{1,2,0:T(8,128)(2,1)S(1)}, f32[2,1024,2,64]{1,3,2,0:T(8,128)S(1)}, f32[2,...) while((s32[]{:T(128)}, ...), condition=%wide.region_4.5_spmd.clone.clone.clone, body=%wide.region_1.4_spmd.clone.clone.clone.sunk | while | flops 551846912 | bytes 23742296 | solution.py:290
  170.4 8.6 fusion.376
  187.4 8.6 fusion.376
  230.9 14.6 all_to_all.114
  253.7 241.7 %while.191 = (s32[]{:T(128)}, bf16[2,1024,384]{1,2,0:T(8,128)(2,1)}, f32[1,640]{1,0:T(1,128)S(1)}, f32[2,1024,384]{1,2,0:T(8,128)}, f32[2,1024,256]{1,2,0:T(8,12...) while((s32[]{:T(128)}, bf16[2,1024,384]{1,2,0:T(8,128)(2,1)}, ...), condition=%wide.region_10.11_spmd, body=%wide.region_5.10_spmd.sunk | while | flops 715629568 | bytes 55300712 | solution.py:291
  269.5 101.5 %while.197 = (s32[]{:T(128)}, f32[6,64,128]{2,1,0:T(8,128)}, f32[4,256,6,64]{1,0,3,2:T(4,128)}, f32[4,256,6,64]{1,0,3,2:T(4,128)}, f32[4,256,128]{2,1,0:T(8,128)...) while((s32[]{:T(128)}, f32[6,64,128]{2,1,0:T(8,128)}, ...), condition=%wide.region_9.9_spmd.clone, body=%wide.region_6.8_spmd.clone.sunk | while | flops 706923520 | bytes 8340415 | solution.py:111
  284.6 9.5 dynamic_update_slice.191
  310.2 9.5 dynamic_update_slice.191
  335.8 9.5 dynamic_update_slice.191
  361.4 9.5 dynamic_update_slice.191
  390.3 101.5 %while.197 = (s32[]{:T(128)}, f32[6,64,128]{2,1,0:T(8,128)}, f32[4,256,6,64]{1,0,3,2:T(4,128)}, f32[4,256,6,64]{1,0,3,2:T(4,128)}, f32[4,256,128]{2,1,0:T(8,128)...) while((s32[]{:T(128)}, f32[6,64,128]{2,1,0:T(8,128)}, ...), condition=%wide.region_9.9_spmd.clone, body=%wide.region_6.8_spmd.clone.sunk | while | flops 706923520 | bytes 8340415 | solution.py:111
  405.5 9.5 dynamic_update_slice.191
  431.1 9.5 dynamic_update_slice.191
  456.7 9.5 dynamic_update_slice.191
  482.3 9.5 dynamic_update_slice.191
  506.1 8.0 all_to_all.115
  551.9 57.9 %all-reduce.24.cloned.1.call-done = bf16[1024,1024]{1,0:T(8,128)(2,1)} async-done(((bf16[1024,1024]{1,0:T(8,128)(2,1)}), bf16[1024,1024]{1,0:T(8,128)(2,1)}) %all-reduce.24.cloned.1.call-update) | async-done | bytes 2097168 | tf_op jit(solution)/shard_map/psum | solution.py:328
  614.4 39.0 %all-gather.19.cloned.1.call-done = bf16[1024,1024]{1,0:T(8,128)(2,1)} async-done(((bf16[64,1024]{1,0:T(8,128)(2,1)}), bf16[1024,1024]{1,0:T(8,128)(2,1)}) %all-gather.19.cloned.1.call-update) | async-done | bytes 2097168 | tf_op jit(solution)/shard_map/all_gather | solution.py:192
  659.9 36.1 %all-gather.17.cloned.1.call-done = bf16[1024,1024]{1,0:T(8,128)(2,1)} async-done(((bf16[64,1024]{1,0:T(8,128)(2,1)}), bf16[1024,1024]{1,0:T(8,128)(2,1)}) %all-gather.17.cloned.1.call-update) | async-done | bytes 2097168 | tf_op jit(solution)/shard_map/all_gather | solution.py:191
  702.5 36.1 %all-gather.21.cloned.1.call-done = bf16[1024,1024]{0,1:T(8,128)(2,1)} async-done(((bf16[1024,64]{0,1:T(8,128)(2,1)}), bf16[1024,1024]{0,1:T(8,128)(2,1)}) %all-gather.21.cloned.1.call-update) | async-done | bytes 2097168 | tf_op jit(solution)/shard_map/all_gather | solution.py:195
  738.6 9.9 multiply_convert_fusion
  758.1 104.9 %all-reduce.26.cloned.1.call-done = f32[1024,1024]{1,0:T(8,128)} async-done(((f32[1024,1024]{1,0:T(8,128)}), f32[1024,1024]{1,0:T(8,128)}) %all-reduce.26.cloned.1.call-update) | async-done | bytes 4194320 | tf_op jit(solution)/shard_map/psum | solution.py:382
  881.1 68.9 %while.192 = (s32[]{:T(128)}, bf16[2,1024,2,64]{1,3,2,0:T(8,128)(2,1)}, bf16[2,1024,64]{1,2,0:T(8,128)(2,1)}, bf16[2,1024,64]{1,2,0:T(8,128)(2,1)}, f32[2,1024,2...) while((s32[]{:T(128)}, ...), condition=%wide.region_22.24_spmd.clone, body=%wide.region_16.23_spmd.clone.sunk | while | flops 1394906240 | bytes 121602872 | solution.py:290
  950.4 7.7 multiply_convert_fusion.3
  975.4 588.5 %while.195 = (s32[]{:T(128)}, f32[4,384]{1,0:T(4,128)}, f32[4,256]{1,0:T(4,128)}, f32[6]{0:T(128)}, f32[6]{0:T(128)}, /*index=5*/f32[6]{0:T(128)S(1)}, bf16[2,10...) while((s32[]{:T(128)}, f32[4,384]{1,0:T(4,128)}, ...), condition=%wide.region_51.53_spmd.clone, body=%wide.region_25.52_spmd.clone.sunk | while | flops 1848495104 | bytes 168048208 | solution.py:291
  997.3 24.8 while.198
  1027.6 208.5 %while.199 = (s32[]{:T(128)}, f32[6,64,128]{2,1,0:T(8,128)}, f32[4,256,6,64]{1,0,3,2:T(4,128)}, f32[4,256,128]{2,1,0:T(8,128)}, f32[4,256,128]{2,1,0:T(8,128)}, ...) while((s32[]{:T(128)}, f32[6,64,128]{2,1,0:T(8,128)}, ...), condition=%wide.region_42.43_spmd.clone, body=%wide.region_30.42_spmd.clone.sunk | while | flops 1669238272 | bytes 15044663 | solution.py:111
  1056.7 7.5 reduce-window.84
  1069.6 9.5 dynamic_update_slice.190
  1109.1 7.5 reduce-window.84
  1121.9 9.5 dynamic_update_slice.190
  1161.4 7.5 reduce-window.84
  1174.3 9.5 dynamic_update_slice.190
  1226.6 9.5 dynamic_update_slice.190
  1250.1 8.1 broadcast_multiply_fusion.7
  1287.3 24.8 while.198
  1317.6 208.5 %while.199 = (s32[]{:T(128)}, f32[6,64,128]{2,1,0:T(8,128)}, f32[4,256,6,64]{1,0,3,2:T(4,128)}, f32[4,256,128]{2,1,0:T(8,128)}, f32[4,256,128]{2,1,0:T(8,128)}, ...) while((s32[]{:T(128)}, f32[6,64,128]{2,1,0:T(8,128)}, ...), condition=%wide.region_42.43_spmd.clone, body=%wide.region_30.42_spmd.clone.sunk | while | flops 1669238272 | bytes 15044663 | solution.py:111
  1359.6 9.5 dynamic_update_slice.190
  1411.9 9.5 dynamic_update_slice.190
  1464.2 9.5 dynamic_update_slice.190
  1516.6 9.5 dynamic_update_slice.190
  1540.8 8.1 broadcast_multiply_fusion.7
  1595.7 8.5 copy.733
  1608.9 7.8 all_to_all.120
  1621.4 8.6 copy.734
  1711.8 103.7 %all-reduce.28.cloned.1.call-done = (bf16[1024,1024]{1,0:T(8,128)(2,1)}, bf16[1024,1024]{1,0:T(8,128)(2,1)}, bf16[1024,256]{1,0:T(8,128)(2,1)}) async-done(((bf16[1024,1024]{1,0:T(8,128)(2,1)}, bf16[1024,1024]{1,0:T(8,128)(2,1)}, bf16[1024,256]{1,0:T(8,128)(2,1)}), (bf16[1024,1024]{1,0:T(8,128)(2,1)}, bf16[1024,1024]{1,0:T(8,128)(2,1)}, bf16[1024,256]{1,0:T(8,128)(2,1)})) %all-reduce.28.cloned.1.call-update) | async-done | bytes 4718608 | tf_op jit(solution)/shard_map/psum | solution.py:341
  1824.4 61.3 %all-reduce.18 = (f32[1024]{0:T(1024)}, f32[1024]{0:T(1024)}, f32[12]{0:T(128)}, f32[12]{0:T(128)}, f32[12]{0:T(128)}, /*index=5*/f32[4,768]{1,0:T(4,128)}, f32[4,256]{1,0:T(4,128)}) all-reduce(f32[1024]{0:T(1024)S(1)} %get-tuple-element.2049, f32[1024]{0:T(1024)S(1)} %copy-done.120, ...), channel_id=1, replica_groups=mesh['dp'=8,'ctx'=2,'tp'=2] {'dp','ctx'}, use_global_device_ids=true, to_apply=%region_57.59 | all-reduce | flops 6180 | bytes 47392 | tf_op jit(solution)/shard_map/psum | solution.py:510
  1885.7 8.3 fusion.166
  1894.1 40.4 %reduce-scatter.28.cloned.1.call-done = f32[64,64]{1,0:T(8,128)} async-done(((f32[1024,64]{1,0:T(8,128)}), f32[64,64]{1,0:T(8,128)}) %reduce-scatter.28.cloned.1.call-update) | async-done | bytes 16400 | tf_op jit(solution)/shard_map/reduce_scatter | solution.py:521
  1934.5 60.9 %reduce-scatter.30.cloned.1.call-done = f32[256,64]{0,1:T(8,128)} async-done(((f32[256,1024]{0,1:T(8,128)}), f32[256,64]{0,1:T(8,128)}) %reduce-scatter.30.cloned.1.call-update) | async-done | bytes 65552 | tf_op jit(solution)/shard_map/reduce_scatter | solution.py:538
  1995.4 60.6 %reduce-scatter.24.cloned.1.call-done = f32[64,256]{1,0:T(8,128)} async-done(((f32[1024,256]{1,0:T(8,128)}), f32[64,256]{1,0:T(8,128)}) %reduce-scatter.24.cloned.1.call-update) | async-done | bytes 65552 | tf_op jit(solution)/shard_map/reduce_scatter | solution.py:515
  2056.0 76.3 %reduce-scatter.44.cloned.1.call-done = f32[1024,64]{0,1:T(8,128)} async-done(((f32[1024,1024]{0,1:T(8,128)}), f32[1024,64]{0,1:T(8,128)}) %reduce-scatter.44.cloned.1.call-update) | async-done | bytes 262160 | tf_op jit(solution)/shard_map/reduce_scatter | solution.py:540
  2132.3 75.8 %reduce-scatter.40.cloned.1.call-done = f32[64,1024]{1,0:T(8,128)} async-done(((f32[1024,1024]{1,0:T(8,128)}), f32[64,1024]{1,0:T(8,128)}) %reduce-scatter.40.cloned.1.call-update) | async-done | bytes 262160 | tf_op jit(solution)/shard_map/reduce_scatter | solution.py:536
  2208.1 76.4 %reduce-scatter.42.cloned.1.call-done = f32[64,1024]{1,0:T(8,128)} async-done(((f32[1024,1024]{1,0:T(8,128)}), f32[64,1024]{1,0:T(8,128)}) %reduce-scatter.42.cloned.1.call-update) | async-done | bytes 262160 | tf_op jit(solution)/shard_map/reduce_scatter | solution.py:537
  2284.5 69.6 %reduce-scatter.38.cloned.1.call-done = f32[768,64]{0,1:T(8,128)} async-done(((f32[768,1024]{0,1:T(8,128)}), f32[768,64]{0,1:T(8,128)}) %reduce-scatter.38.cloned.1.call-update) | async-done | bytes 196624 | tf_op jit(solution)/shard_map/reduce_scatter | solution.py:539
  2354.1 69.7 %reduce-scatter.34.cloned.1.call-done = f32[64,768]{1,0:T(8,128)} async-done(((f32[1024,768]{1,0:T(8,128)}), f32[64,768]{1,0:T(8,128)}) %reduce-scatter.34.cloned.1.call-update) | async-done | bytes 196624 | tf_op jit(solution)/shard_map/reduce_scatter | solution.py:527
  2423.8 69.5 %reduce-scatter.32.cloned.1.call-done = f32[64,768]{1,0:T(8,128)} async-done(((f32[1024,768]{1,0:T(8,128)}), f32[64,768]{1,0:T(8,128)}) %reduce-scatter.32.cloned.1.call-update) | async-done | bytes 196624 | tf_op jit(solution)/shard_map/reduce_scatter | solution.py:524
  2493.3 60.6 %reduce-scatter.36.cloned.1.call-done = f32[64,256]{1,0:T(8,128)} async-done(((f32[1024,256]{1,0:T(8,128)}), f32[64,256]{1,0:T(8,128)}) %reduce-scatter.36.cloned.1.call-update) | async-done | bytes 65552 | tf_op jit(solution)/shard_map/reduce_scatter | solution.py:530
  (1676 shorter events, 1030.1 us)
Async XLA Ops:
  7.2 212.6 %copy-start = (f32[4,768]{1,0:T(4,128)S(1)}, f32[4,768]{1,0:T(4,128)}, u32[]{:S(2)}) copy-start(f32[4,768]{1,0:T(4,128)} %param.52) | copy-start | bytes 36868
  7.2 28.3 %copy-start.7 = (bf16[2,512,1024]{2,1,0:T(8,128)(2,1)S(1)}, bf16[2,512,1024]{2,1,0:T(8,128)(2,1)}, u32[]{:S(2)}) copy-start(bf16[2,512,1024]{2,1,0:T(8,128)(2,1)} %param.37) | copy-start | bytes 6291460
  7.2 28.3 %copy-start.112 = (f32[1024]{0:T(1024)S(1)}, f32[1024]{0:T(1024)}, u32[]{:S(2)}) copy-start(f32[1024]{0:T(1024)} %param.39) | copy-start | bytes 12292
  7.2 213.2 %all-gather.13.cloned.1.call-start = ((), (), s32[]{:S(2)}) async-start(), calls=%async_computation.27 | async-start | bytes 1572864 | tf_op jit(solution)/shard_map/all_gather | solution.py:243
  10.7 26.1 %copy-start.110 = (f32[1024]{0:T(1024)}, f32[1024]{0:T(1024)S(1)}, u32[]{:S(2)}) copy-start(f32[1024]{0:T(1024)S(1)} %rsqrt.23) | copy-start | bytes 12292
  38.4 184.8 %all-gather.11.cloned.1.call-start = ((), (), s32[]{:S(2)}) async-start(), calls=%async_computation.26 | async-start | bytes 1671168 | tf_op jit(solution)/shard_map/all_gather | solution.py:187
  39.2 497.6 %all-gather.9.cloned.1.call-start = ((), (), s32[]{:S(2)}) async-start(), calls=%async_computation.25 | async-start | bytes 1671168 | tf_op jit(solution)/shard_map/all_gather | solution.py:188
  62.0 28.6 %copy-start.121 = (bf16[64,64]{1,0:T(8,128)(2,1)S(1)}, bf16[64,64]{1,0:T(8,128)(2,1)}, u32[]{:S(2)}) copy-start(bf16[64,64]{1,0:T(8,128)(2,1)} %param.42) | copy-start | bytes 24580
  62.0 46.7 %copy-start.122 = (bf16[64,64]{1,0:T(8,128)(2,1)S(1)}, bf16[64,64]{1,0:T(8,128)(2,1)}, u32[]{:S(2)}) copy-start(bf16[64,64]{1,0:T(8,128)(2,1)} %param.43) | copy-start | bytes 24580
  62.0 66.8 %copy-start.115 = (bf16[256,64]{0,1:T(8,128)(2,1)S(1)}, bf16[256,64]{0,1:T(8,128)(2,1)}, u32[]{:S(2)}) copy-start(bf16[256,64]{0,1:T(8,128)(2,1)} %param.44) | copy-start | bytes 98308
  62.0 88.0 %copy-start.23 = (bf16[1024,1024]{1,0:T(8,128)(2,1)S(1)}, bf16[1024,1024]{1,0:T(8,128)(2,1)}, u32[]{:S(2)}) copy-start(bf16[1024,1024]{1,0:T(8,128)(2,1)} %copy-done.22) | copy-start | bytes 6291460
  63.4 94.4 %all-to-all-start = ((bf16[2,512,4,64]{1,0,3,2:T(2,128)(2,1)}), bf16[2,512,4,64]{1,0,3,2:T(2,128)(2,1)S(1)}, u32[]{:S(2)}, u32[]{:S(2)}) async-start(bf16[2,512,4,64]{1,0,3,2:T(2,128)(2,1)} %reshape.883), calls=%async_computation | async-start | bytes 1048576 | tf_op jit(solution)/shard_map/all_to_all | solution.py:208
  66.9 476.4 %all-gather.15.cloned.1.call-start = ((), (), s32[]{:S(2)}) async-start(), calls=%async_computation.28 | async-start | bytes 1671168 | tf_op jit(solution)/shard_map/all_gather | solution.py:194
  90.6 61.5 %copy-start.77 = (bf16[1024,12]{0,1:T(8,128)(2,1)}, bf16[1024,12]{0,1:T(8,128)(2,1)S(1)}, u32[]{:S(2)}) copy-start(bf16[1024,12]{0,1:T(8,128)(2,1)S(1)} %reshape.952) | copy-start | bytes 73732
  108.7 43.4 %copy-start.50 = (bf16[1024,64]{1,0:T(8,128)(2,1)}, bf16[1024,64]{1,0:T(8,128)(2,1)S(1)}, u32[]{:S(2)}) copy-start(bf16[1024,64]{1,0:T(8,128)(2,1)S(1)} %all_gather.60) | copy-start | bytes 393220
  128.8 25.3 copy-start.52
  157.8 49.7 %all-to-all-start.3 = ((bf16[2,512,12,1]{1,0,3,2:T(2,128)(2,1)}), bf16[2,512,12,1]{1,0,3,2:T(2,128)(2,1)}, u32[]{:S(2)}, u32[]{:S(2)}) async-start(bf16[2,512,12,1]{1,0,3,2:T(2,128)(2,1)} %bitcast.17), calls=%async_computation.3 | async-start | bytes 49152 | tf_op jit(solution)/shard_map/all_to_all | solution.py:222
  201.1 15.0 copy-start.20
  201.1 15.0 copy-start.29
  207.4 6.2 all-to-all-start.1
  211.8 398.0 %all-reduce.24.cloned.1.call-start = ((), (), s32[]{:S(2)}) async-start(), calls=%async_computation.29 | async-start | bytes 4194304 | tf_op jit(solution)/shard_map/psum | solution.py:328
  549.2 60.5 %copy-start.8 = (bf16[2,512,1024]{2,1,0:T(8,128)(2,1)S(1)}, bf16[2,512,1024]{2,1,0:T(8,128)(2,1)}, u32[]{:S(2)}) copy-start(bf16[2,512,1024]{2,1,0:T(8,128)(2,1)} %param.37) | copy-start | bytes 6291460
  549.3 63.0 %copy-start.103 = (f32[1024]{0:T(1024)S(1)}, f32[1024]{0:T(1024)}, u32[]{:S(2)}) copy-start(f32[1024]{0:T(1024)} %param.40) | copy-start | bytes 12292
  549.3 104.1 %all-gather.19.cloned.1.call-start = ((), (), s32[]{:S(2)}) async-start(), calls=%async_computation.31 | async-start | bytes 2228224 | tf_op jit(solution)/shard_map/all_gather | solution.py:192
  549.9 146.2 %all-gather.17.cloned.1.call-start = ((), (), s32[]{:S(2)}) async-start(), calls=%async_computation.30 | async-start | bytes 2228224 | tf_op jit(solution)/shard_map/all_gather | solution.py:191
  550.6 188.0 %all-gather.21.cloned.1.call-start = ((), (), s32[]{:S(2)}) async-start(), calls=%async_computation.32 | async-start | bytes 2228224 | tf_op jit(solution)/shard_map/all_gather | solution.py:195
  551.4 311.6 %all-reduce.26.cloned.1.call-start = ((), (), s32[]{:S(2)}) async-start(), calls=%async_computation.33 | async-start | bytes 8388608 | tf_op jit(solution)/shard_map/psum | solution.py:382
  612.3 255.8 %copy-start.93 = (f32[1024]{0:T(1024)}, f32[1024]{0:T(1024)S(1)}, u32[]{:S(2)}) copy-start(f32[1024]{0:T(1024)S(1)} %fusion.180) | copy-start | bytes 12292
  756.2 891.1 %reduce-scatter.18.cloned.1.call-start = ((), (), s32[]{:S(2)}) async-start(), calls=%async_computation.34 | async-start | bytes 393216 | tf_op jit(solution)/shard_map/reduce_scatter | solution.py:456
  950.0 698.3 %reduce-scatter.20.cloned.1.call-start = ((), (), s32[]{:S(2)}) async-start(), calls=%async_computation.35 | async-start | bytes 393216 | tf_op jit(solution)/shard_map/reduce_scatter | solution.py:459
  972.3 685.4 %reduce-scatter.22.cloned.1.call-start = ((), (), s32[]{:S(2)}) async-start(), calls=%async_computation.36 | async-start | bytes 1572864 | tf_op jit(solution)/shard_map/reduce_scatter | solution.py:462
  997.3 25.0 copy-start.17
  1049.3 16.7 copy-start.35
  1052.6 13.4 copy-start.36
  1101.6 16.7 copy-start.35
  1105.0 13.4 copy-start.36
  1154.0 16.7 copy-start.35
  1157.3 13.4 copy-start.36
  1206.3 16.7 copy-start.35
  1209.7 13.4 copy-start.36
  1287.3 25.0 copy-start.17
  1339.3 16.7 copy-start.35
  1391.6 16.7 copy-start.35
  1395.0 13.4 copy-start.36
  1444.0 16.7 copy-start.35
  1496.3 16.7 copy-start.35
  1563.9 146.4 %reduce-scatter.46.cloned.1.call-start = ((), (), s32[]{:S(2)}) async-start(), calls=%async_computation.48 | async-start | bytes 557056
  1637.4 178.1 %all-reduce.28.cloned.1.call-start = ((), (), s32[]{:S(2)}) async-start(), calls=%async_computation.49 | async-start | bytes 9437184 | tf_op jit(solution)/shard_map/psum | solution.py:341
  1657.7 236.3 %reduce-scatter.26.cloned.1.call-start = ((), (), s32[]{:S(2)}) async-start(), calls=%async_computation.38 | async-start | bytes 557056 | tf_op jit(solution)/shard_map/reduce_scatter | solution.py:518
  1660.2 274.3 %reduce-scatter.28.cloned.1.call-start = ((), (), s32[]{:S(2)}) async-start(), calls=%async_computation.39 | async-start | bytes 557056 | tf_op jit(solution)/shard_map/reduce_scatter | solution.py:521
  1661.8 333.6 %reduce-scatter.30.cloned.1.call-start = ((), (), s32[]{:S(2)}) async-start(), calls=%async_computation.40 | async-start | bytes 1114112 | tf_op jit(solution)/shard_map/reduce_scatter | solution.py:538
  1665.4 390.6 %reduce-scatter.24.cloned.1.call-start = ((), (), s32[]{:S(2)}) async-start(), calls=%async_computation.37 | async-start | bytes 1114112 | tf_op jit(solution)/shard_map/reduce_scatter | solution.py:515
  1667.2 465.0 %reduce-scatter.44.cloned.1.call-start = ((), (), s32[]{:S(2)}) async-start(), calls=%async_computation.47 | async-start | bytes 4456448 | tf_op jit(solution)/shard_map/reduce_scatter | solution.py:540
  1673.9 534.2 %reduce-scatter.40.cloned.1.call-start = ((), (), s32[]{:S(2)}) async-start(), calls=%async_computation.45 | async-start | bytes 4456448 | tf_op jit(solution)/shard_map/reduce_scatter | solution.py:536
  1680.9 603.6 %reduce-scatter.42.cloned.1.call-start = ((), (), s32[]{:S(2)}) async-start(), calls=%async_computation.46 | async-start | bytes 4456448 | tf_op jit(solution)/shard_map/reduce_scatter | solution.py:537
  1687.6 666.5 %reduce-scatter.38.cloned.1.call-start = ((), (), s32[]{:S(2)}) async-start(), calls=%async_computation.44 | async-start | bytes 3342336 | tf_op jit(solution)/shard_map/reduce_scatter | solution.py:539
  1693.3 730.5 %reduce-scatter.34.cloned.1.call-start = ((), (), s32[]{:S(2)}) async-start(), calls=%async_computation.42 | async-start | bytes 3342336 | tf_op jit(solution)/shard_map/reduce_scatter | solution.py:527
  1698.9 794.4 %reduce-scatter.32.cloned.1.call-start = ((), (), s32[]{:S(2)}) async-start(), calls=%async_computation.41 | async-start | bytes 3342336 | tf_op jit(solution)/shard_map/reduce_scatter | solution.py:524
  1703.9 850.0 %reduce-scatter.36.cloned.1.call-start = ((), (), s32[]{:S(2)}) async-start(), calls=%async_computation.43 | async-start | bytes 1114112 | tf_op jit(solution)/shard_map/reduce_scatter | solution.py:530
  1819.2 66.5 %copy-start.107 = (f32[1,4,2,128]{3,1,2,0:T(4,128)S(1)}, f32[1,4,2,128]{3,1,2,0:T(4,128)}, u32[]{:S(2)}) copy-start(f32[1,4,2,128]{3,1,2,0:T(4,128)} %copy-done.106) | copy-start | bytes 12292
  1819.2 66.5 %copy-start.94 = (f32[1024]{0:T(1024)S(1)}, f32[1024]{0:T(1024)}, u32[]{:S(2)}) copy-start(f32[1024]{0:T(1024)} %copy-done.93) | copy-start | bytes 12292
  1819.2 66.5 %copy-start.104 = (f32[1024]{0:T(1024)S(1)}, f32[1024]{0:T(1024)}, u32[]{:S(2)}) copy-start(f32[1024]{0:T(1024)} %param.40) | copy-start | bytes 12292
  1819.2 66.5 %copy-start.109 = (f32[1024]{0:T(1024)S(1)}, f32[1024]{0:T(1024)}, u32[]{:S(2)}) copy-start(f32[1024]{0:T(1024)} %copy-done.108) | copy-start | bytes 12292
  1885.7 668.1 %copy-start.1 = (f32[4,768]{1,0:T(4,128)S(1)}, f32[4,768]{1,0:T(4,128)}, u32[]{:S(2)}) copy-start(f32[4,768]{1,0:T(4,128)} %param.52) | copy-start | bytes 36868
  (250 other events, 1106.5 us)
Sparse Core Ops, SparseCore 0:
  38.5 6.3 all-gather.12
  47.2 40.9 all-gather.10
  90.5 39.7 all-gather.8
  132.5 38.8 all-gather.14
  549.4 60.3 all-reduce.23
  612.0 41.3 all-gather.18
  655.8 40.1 all-gather.16
  698.4 40.1 all-gather.20
  756.3 106.6 all-reduce.25
  950.1 7.6 reduce-scatter.17
  972.4 7.6 reduce-scatter.19
  1564.0 8.5 reduce-scatter.21
  1637.5 55.7 reduce-scatter.45
  1696.5 119.0 all-reduce.27
  1819.9 55.7 reduce-scatter.25
  1879.7 54.7 reduce-scatter.27
  1939.0 56.3 reduce-scatter.29
  1999.4 56.4 reduce-scatter.23
  2060.9 71.3 reduce-scatter.43
  2136.6 71.5 reduce-scatter.39
  2213.1 71.4 reduce-scatter.41
  2288.9 65.1 reduce-scatter.37
  2358.5 65.2 reduce-scatter.33
  2428.0 65.1 reduce-scatter.31
  2497.5 56.3 reduce-scatter.35
where the time goes:
time: 2580 us; the launch traced here: 2560 us
  waiting for transfers between devices  1040 us (40%)
  local copies, waits for them, and re-layouts  553 us (21%)
  matrix products  391 us (15%)
  other arithmetic  290 us (11%)
  blocking collectives  243 us (9%)
    dynamic_update_slice x40, local copies, waits for them, and re-layouts, ssd_one(): lax.scan(jax.checkpoint(block_step), start_state, pieces)  171 us
    another operation x88, other arithmetic  130 us
    psum x1, waiting for transfers between devices, per_device(): lax.psum(dot_back(grad_gate, full_gate) + dot_back(grad_up, full_up), 'tp')  105 us
    psum x1, waiting for transfers between devices, per_device(): lax.psum(plain_dot(inner_rows, full_down).astype(jnp.bfloat16), 'tp')  104 us
    dot_general x24, matrix products, block_step(): jnp.einsum('tsh,shp->thp', mixing, ssm_heads, precision=TOP_PRECISION)  79.7 us
    reduce_scatter x1, waiting for transfers between devices, per_device(): lax.psum_scatter(grad_w_up, ('dp', 'ctx'), scatter_dimension=0, tiled=True)  76.4 us
    reduce_scatter x1, waiting for transfers between devices, per_device(): lax.psum_scatter(grad_w_down, ('dp', 'ctx'), scatter_dimension=1, tiled=T...  76.3 us
    reduce_scatter x1, waiting for transfers between devices, per_device(): lax.psum_scatter(grad_w_gate, ('dp', 'ctx'), scatter_dimension=0, tiled=T...  75.8 us
  transfers between devices with their start and end apart: 28, of which 17 were waited for; matrix products, arithmetic and copies ran while one was open for 43% of the time, Pallas kernels for 0%

commit v1 on v0

v1 whole, which is shorter than its diff:
```python
import jax
import jax.numpy as jnp
from jax import lax
from jax.sharding import PartitionSpec as P

QUERY_HEADS = 8
KEY_VALUE_HEADS = 2
ATTN_HEAD_SIZE = 64
MIXER_HEAD_SIZE = 64
NS = 128
CONV_TAPS = 4
SPAN = 256


TOP_PRECISION = lax.Precision.HIGHEST
EPSILON = 1e-05
ROPE_BASE = 10000.0


def rms_scale(values, gain_row):
    return (
        values * lax.rsqrt(jnp.mean(values * values, axis=-1, keepdims=True) + EPSILON) * gain_row
    )


def rope_turn(values):
    half_dim = values.shape[-1] // 2
    position = jnp.arange(values.shape[0], dtype=jnp.float32)
    frequency = ROPE_BASE ** (-jnp.arange(half_dim, dtype=jnp.float32) / half_dim)
    angles = position[:, None] * frequency[None, :]
    cosine = jnp.cos(angles)[:, None, :]
    sine_part = jnp.sin(angles)[:, None, :]
    first_half = values[..., :half_dim]
    second_half = values[..., half_dim:]
    return jnp.concatenate(
        [
            first_half * cosine - second_half * sine_part,
            second_half * cosine + first_half * sine_part,
        ],
        axis=-1,
    )


def attend(queries, key_rows, value_rows):
    batch, length, kv_count, group, head_dim = queries.shape
    turn = jax.vmap(rope_turn)
    turned_queries = turn(
        queries.reshape(batch, length, kv_count * group, head_dim).astype(jnp.float32)
    ).astype(jnp.bfloat16)
    turned_queries = turned_queries.reshape(queries.shape)
    turned_keys = turn(key_rows.astype(jnp.float32)).astype(jnp.bfloat16)
    scores = jnp.einsum(
        "bqcgd,bkcd->bcgqk", turned_queries, turned_keys, preferred_element_type=jnp.float32
    ) * head_dim ** (-0.5)
    positions = jnp.arange(length)
    causal = positions[None, :] <= positions[:, None]
    scores = jnp.where(causal, scores, -1e30)
    weights = jax.nn.softmax(scores, axis=-1).astype(jnp.bfloat16)
    return jnp.einsum(
        "bcgqk,bkcd->bqcgd", weights, value_rows, preferred_element_type=jnp.float32
    )


def bf(values):
    return values.astype(jnp.bfloat16)


def ein(form, *operands):
    return jnp.einsum(form, *operands, preferred_element_type=jnp.float32)


def conv_silu(values, taps):
    length = values.shape[1]
    tap_count = taps.shape[0]
    padded = jnp.pad(values, ((0, 0), (tap_count - 1, 0), (0, 0))).astype(jnp.float32)
    convolved = taps[0] * padded[:, 0:length]
    for offset in range(1, tap_count):
        convolved = convolved + taps[offset] * padded[:, offset : offset + length]
    return jax.nn.silu(convolved)


def ssd(mixer_input, shared_in, dt_raw, dt_shift, log_rate, skip_gain, conv_ssm, conv_common):
    batch, length, head_count = dt_raw.shape
    head_dim = mixer_input.shape[-1] // head_count
    state_dim = shared_in.shape[-1] // 2
    blocks = length // SPAN
    heads_last = conv_silu(mixer_input, conv_ssm).reshape(
        batch, blocks, SPAN, head_count, head_dim
    )
    ssm_heads = heads_last.transpose(0, 1, 3, 2, 4)
    common = conv_silu(shared_in, conv_common).reshape(batch, blocks, SPAN, 2 * state_dim)
    write_rows = bf(common[..., :state_dim])
    read_rows = bf(common[..., state_dim:])
    step_size = jax.nn.softplus(dt_raw.astype(jnp.float32) + dt_shift)
    step_size = step_size.reshape(batch, blocks, SPAN, head_count).transpose(0, 1, 3, 2)
    log_decay = -step_size * jnp.exp(log_rate)[:, None]
    positions = jnp.arange(SPAN)
    lower_mask = positions[None, :] <= positions[:, None]
    cumulative = jnp.einsum(
        "bkhs,ts->bkht", log_decay, lower_mask.astype(jnp.float32), precision=TOP_PRECISION
    )
    log_gap = cumulative[..., :, None] - cumulative[..., None, :]
    decay_table = jnp.exp(jnp.where(lower_mask, log_gap, -1e30))
    pairing = ein("bktn,bksn->bkts", read_rows, write_rows)
    mixing = bf(pairing[:, :, None] * decay_table * step_size[..., None, :])
    heads_low = bf(ssm_heads)
    within = ein("bkhts,bkhsp->bkhtp", mixing, heads_low)
    last = cumulative[..., -1]
    tail_weight = jnp.exp(last[..., None] - cumulative) * step_size
    added = ein("bkhsp,bksn->bkhpn", bf(ssm_heads * tail_weight[..., None]), write_rows)
    states = [jnp.zeros_like(added[:, 0])]
    for block in range(blocks - 1):
        states.append(jnp.exp(last[:, block])[..., None, None] * states[-1] + added[:, block])
    carry_state = jnp.stack(states, axis=1)
    carried = ein("bktn,bkhpn->bkhtp", read_rows, bf(carry_state)) * jnp.exp(cumulative)[..., None]
    result = within + carried + skip_gain[:, None, None] * ssm_heads
    return bf(result).transpose(0, 1, 3, 2, 4).reshape(batch, length, head_count * head_dim)


def plain_dot(operand, weight_matrix):
    return jnp.dot(operand, weight_matrix, preferred_element_type=jnp.float32)


def dot_back(operand, weight_matrix):
    return lax.dot_general(
        operand, weight_matrix, (((1,), (1,)), ((), ())), preferred_element_type=jnp.float32
    )


def dot_left(operand, weight_matrix):
    return lax.dot_general(
        operand, weight_matrix, (((0,), (0,)), ((), ())), preferred_element_type=jnp.float32
    )


def gate_silu(gate_in, other_rows):
    return jax.nn.silu(gate_in) * other_rows


SWAP = [(0, 1), (1, 0)]


def take_sequences(values):
    me = lax.axis_index("ctx")
    count, half, width = values.shape
    share = count // 2
    mine = lax.dynamic_slice_in_dim(values, me * share, share, 0)
    sent = lax.dynamic_slice_in_dim(values, (1 - me) * share, share, 0)
    got = lax.ppermute(sent, "ctx", SWAP)
    whole = jnp.zeros((share, 2 * half, width), values.dtype)
    whole = lax.dynamic_update_slice_in_dim(whole, mine, me * half, 1)
    return lax.dynamic_update_slice_in_dim(whole, got, (1 - me) * half, 1)


def give_positions(values):
    me = lax.axis_index("ctx")
    share, length, width = values.shape
    half = length // 2
    mine = lax.dynamic_slice_in_dim(values, me * half, half, 1)
    sent = lax.dynamic_slice_in_dim(values, (1 - me) * half, half, 1)
    got = lax.ppermute(sent, "ctx", SWAP)
    whole = jnp.zeros((2 * share, half, width), values.dtype)
    whole = lax.dynamic_update_slice_in_dim(whole, mine, me * share, 0)
    return lax.dynamic_update_slice_in_dim(whole, got, (1 - me) * share, 0)


def tp_sum(values):
    own = lax.optimization_barrier(bf(values))
    other = lax.ppermute(own, "tp", SWAP)
    return own.astype(jnp.float32) + other.astype(jnp.float32)


def gather_rows(shard):
    rows, columns = shard.shape
    over_dp = lax.all_gather(shard, "dp", axis=0, tiled=False)
    both = lax.all_gather(over_dp, "ctx", axis=1, tiled=True)
    return both.reshape(-1, columns)


def split_rows(values, rows):
    me = lax.axis_index("ctx")
    parts = values.reshape(values.shape[0], -1, 2, rows)
    mine = lax.dynamic_index_in_dim(parts, me, 2, False)
    other = lax.dynamic_index_in_dim(parts, 1 - me, 2, False)
    return mine.reshape(values.shape[0], -1), other.reshape(values.shape[0], -1)


def core_sum(left, right, rows):
    mine, other = split_rows(left, rows)
    got = lax.ppermute(bf(dot_left(other, right)), "ctx", SWAP)
    return bf(dot_left(mine, right) + got.astype(jnp.float32))


def dp_scatter(values):
    return lax.psum_scatter(values, "dp", scatter_dimension=0, tiled=True).astype(jnp.float32)


def per_device(
    hidden_in,
    cotangent,
    attn_norm_gain,
    ffn_norm_gain,
    w_query,
    key_weight,
    value_weight,
    w_attn_out,
    mixer_input_weight,
    mixer_gate_weight,
    w_ssm_bc,
    w_ssm_dt,
    dt_bias,
    a_log,
    d_skip,
    input_conv_taps,
    conv_bc,
    mixer_output_weight,
    w_gate,
    w_up,
    w_down,
):
    sequence_count, halved_length, model_width = hidden_in.shape
    tp_index = lax.axis_index("tp")
    batch = sequence_count // 2
    length = halved_length * 2
    count_of_rows = batch * length
    shard_rows = w_query.shape[0]
    q_w = w_query.shape[1]
    kv_w = key_weight.shape[1]
    x_w = mixer_input_weight.shape[1]
    bc_w = w_ssm_bc.shape[1]
    local_mixer = w_ssm_dt.shape[1]
    ff_w = w_gate.shape[1]
    local_kv = kv_w // ATTN_HEAD_SIZE
    group = q_w // kv_w
    dt_w = -(-local_mixer // 128) * 128
    edges = [0]
    for width in (x_w, q_w, bc_w, kv_w, kv_w, dt_w, x_w):
        edges.append(edges[-1] + width)
    gate_at = edges[6]

    in_shard = jnp.concatenate(
        [
            mixer_input_weight,
            w_query,
            w_ssm_bc,
            key_weight,
            value_weight,
            jnp.pad(w_ssm_dt, ((0, 0), (0, dt_w - local_mixer))),
            mixer_gate_weight,
        ],
        axis=1,
    )
    rest_shard = jnp.concatenate(
        [w_attn_out.T, mixer_output_weight.T, w_gate, w_up, w_down.T], axis=1
    )
    full_in = gather_rows(in_shard)
    full_rest = gather_rows(rest_shard)
    out_w = q_w + x_w
    full_out = full_rest[:, :out_w]
    full_gate_up = full_rest[:, out_w : out_w + 2 * ff_w]
    full_down = full_rest[:, out_w + 2 * ff_w :]

    hidden = take_sequences(hidden_in).astype(jnp.float32).reshape(count_of_rows, model_width)
    grad_rows = take_sequences(cotangent).reshape(count_of_rows, model_width)

    normed_full, attn_norm_pull = jax.vjp(rms_scale, hidden, attn_norm_gain)
    normed = bf(normed_full)
    projected = bf(plain_dot(normed, full_in[:, :gate_at]))
    gate_ssm = plain_dot(normed, full_in[:, gate_at:])
    pieces = [projected[:, low:high] for low, high in zip(edges[:6], edges[1:7])]
    mixer_input, queries, shared_rows, key_rows, value_rows, dt_raw = pieces
    dt_raw = dt_raw[:, :local_mixer]

    attended, attend_pull = jax.vjp(
        attend,
        queries.reshape(batch, length, local_kv, group, ATTN_HEAD_SIZE),
        key_rows.reshape(batch, length, local_kv, ATTN_HEAD_SIZE),
        value_rows.reshape(batch, length, local_kv, ATTN_HEAD_SIZE),
    )
    scan_result, ssd_pull = jax.vjp(
        ssd,
        mixer_input.reshape(batch, length, x_w),
        shared_rows.reshape(batch, length, bc_w),
        dt_raw.reshape(batch, length, local_mixer),
        dt_bias,
        a_log,
        d_skip,
        input_conv_taps,
        conv_bc,
    )
    attn_rows = bf(attended).reshape(count_of_rows, q_w)
    mixer_rows = scan_result.reshape(count_of_rows, x_w)
    gated_full, gate_pull = jax.vjp(gate_silu, gate_ssm, mixer_rows.astype(jnp.float32))
    mixed_in = jnp.concatenate([attn_rows, bf(gated_full)], axis=1)
    middle = hidden + tp_sum(dot_back(mixed_in, full_out))
    normed_ffn_full, ffn_norm_pull = jax.vjp(rms_scale, middle, ffn_norm_gain)
    normed_ffn = bf(normed_ffn_full)
    gate_up = plain_dot(normed_ffn, full_gate_up)
    inner_full, inner_pull = jax.vjp(gate_silu, gate_up[:, :ff_w], gate_up[:, ff_w:])
    inner_rows = bf(inner_full)

    grad_inner = plain_dot(grad_rows, full_down)
    grad_gate_full, grad_up_full = inner_pull(grad_inner)
    grad_gate_up = jnp.concatenate([bf(grad_gate_full), bf(grad_up_full)], axis=1)
    grad_ffn_partial = dot_back(grad_gate_up, full_gate_up)
    ffn_gain_part = ffn_norm_pull(grad_ffn_partial)[1]
    grad_middle = grad_rows.astype(jnp.float32) + ffn_norm_pull(tp_sum(grad_ffn_partial))[0]
    ffn_sent = jnp.concatenate(
        [
            core_sum(normed_ffn, grad_gate_up, shard_rows),
            core_sum(grad_rows, inner_rows, shard_rows),
        ],
        axis=1,
    )
    ffn_grads = dp_scatter(ffn_sent)

    grad_mixed = bf(grad_middle)
    out_grads = dp_scatter(core_sum(grad_mixed, mixed_in, shard_rows))
    grad_mixed_in = plain_dot(grad_mixed, full_out)
    grad_attn_rows = grad_mixed_in[:, :q_w]
    grad_gate_ssm, mixer_row_gradient = gate_pull(grad_mixed_in[:, q_w:])

    out_partial = dot_back(inner_rows, full_down)
    output = give_positions(
        bf(middle + tp_sum(out_partial)).reshape(batch, length, model_width)
    )

    grad_queries, grad_keys, grad_values = attend_pull(
        bf(grad_attn_rows)
        .astype(jnp.float32)
        .reshape(batch, length, local_kv, group, ATTN_HEAD_SIZE)
    )
    (
        grad_x,
        grad_shared,
        grad_dt,
        grad_shift,
        grad_rate,
        grad_skip,
        grad_conv_x,
        grad_conv_common,
    ) = ssd_pull(bf(mixer_row_gradient).reshape(batch, length, x_w))
    grad_all = jnp.concatenate(
        [
            grad_x.reshape(count_of_rows, x_w),
            grad_queries.reshape(count_of_rows, q_w),
            grad_shared.reshape(count_of_rows, bc_w),
            grad_keys.reshape(count_of_rows, kv_w),
            grad_values.reshape(count_of_rows, kv_w),
            jnp.pad(
                grad_dt.reshape(count_of_rows, local_mixer), ((0, 0), (0, dt_w - local_mixer))
            ),
            bf(grad_gate_ssm),
        ],
        axis=1,
    )
    in_grads = dp_scatter(core_sum(normed, grad_all, shard_rows))
    partial_in = dot_back(grad_all, full_in)
    attn_gain_part = attn_norm_pull(partial_in)[1]
    grad_hidden_norm = attn_norm_pull(tp_sum(partial_in))[0]
    grad_input = give_positions(
        bf(grad_middle + grad_hidden_norm).reshape(batch, length, model_width)
    )

    own = jnp.concatenate([grad_shift, grad_rate, grad_skip, grad_conv_x.reshape(-1)])
    placed = lax.dynamic_update_slice(
        jnp.zeros((lax.axis_size("tp") * own.shape[0],), jnp.float32),
        own,
        (tp_index * own.shape[0],),
    )
    small = jnp.concatenate(
        [attn_gain_part, ffn_gain_part, grad_conv_common.reshape(-1), placed]
    )
    small_size = small.shape[0]
    small = jnp.pad(small, (0, -small_size % 1024)).reshape(-1, 128)
    small = lax.psum(small, ("dp", "ctx", "tp")).reshape(-1)
    conv_size = conv_bc.size
    tail_at = 2 * model_width + conv_size
    own = lax.dynamic_slice(small, (tail_at + tp_index * own.shape[0],), (own.shape[0],))
    in_parts = [in_grads[:, low:high] for low, high in zip(edges[:7], edges[1:8])]
    shared_grad = in_parts[2] + lax.ppermute(in_parts[2], "tp", SWAP)
    return (
        output,
        grad_input,
        small[:model_width],
        small[model_width : 2 * model_width],
        in_parts[1],
        in_parts[3],
        in_parts[4],
        out_grads[:, :q_w].T,
        in_parts[0],
        in_parts[6],
        shared_grad,
        in_parts[5][:, :local_mixer],
        own[:local_mixer],
        own[local_mixer : 2 * local_mixer],
        own[2 * local_mixer : 3 * local_mixer],
        own[3 * local_mixer :].reshape(input_conv_taps.shape),
        small[2 * model_width : tail_at].reshape(conv_bc.shape),
        out_grads[:, q_w:].T,
        ffn_grads[:, :ff_w],
        ffn_grads[:, ff_w : 2 * ff_w],
        ffn_grads[:, 2 * ff_w :].T,
    )


def solution(mesh):
    in_specs = (
        P("dp", "ctx", None),
        P("dp", "ctx", None),
        P(),
        P(),
        P(("dp", "ctx"), "tp"),
        P(("dp", "ctx"), "tp"),
        P(("dp", "ctx"), "tp"),
        P("tp", ("dp", "ctx")),
        P(("dp", "ctx"), "tp"),
        P(("dp", "ctx"), "tp"),
        P(("dp", "ctx"), None),
        P(("dp", "ctx"), "tp"),
        P("tp"),
        P("tp"),
        P("tp"),
        P(None, "tp"),
        P(),
        P("tp", ("dp", "ctx")),
        P(("dp", "ctx"), "tp"),
        P(("dp", "ctx"), "tp"),
        P("tp", ("dp", "ctx")),
    )
    out_specs = (
        P("dp", "ctx", None),
        P("dp", "ctx", None),
        P(),
        P(),
        P(("dp", "ctx"), "tp"),
        P(("dp", "ctx"), "tp"),
        P(("dp", "ctx"), "tp"),
        P("tp", ("dp", "ctx")),
        P(("dp", "ctx"), "tp"),
        P(("dp", "ctx"), "tp"),
        P(("dp", "ctx"), None),
        P(("dp", "ctx"), "tp"),
        P("tp"),
        P("tp"),
        P("tp"),
        P(None, "tp"),
        P(),
        P("tp", ("dp", "ctx")),
        P(("dp", "ctx"), "tp"),
        P(("dp", "ctx"), "tp"),
        P("tp", ("dp", "ctx")),
    )
    return jax.shard_map(
        per_device, mesh=mesh, in_specs=in_specs, out_specs=out_specs, check_vma=False
    )
```

time: 2580 us -> 719 us (0.28)
  waiting for transfers between devices: 1040 us -> 267 us
  local copies, waits for them, and re-layouts: 553 us -> 122 us
  matrix products: 391 us -> 170 us
  blocking collectives: 243 us -> 40.9 us
  other arithmetic: 290 us -> 88.2 us
    reduce_scatter x14 -> x3, waiting for transfers between devices: 660 us -> 3.35 us  [dp_scatter(): lax.psum_scatter(values, 'dp', scatter_dimension=0, tiled=True)]
    psum x3 -> x0, waiting for transfers between devices: 266 us -> none  [the longest x1 105 us: per_device(): lax.psum(dot_back(grad_gate, full_gate) + dot_back(grad_up, full_up), 'tp')]
    dynamic_update_slice x52 -> x8, local copies, waits for them, and re-layouts: 177 us -> 10.7 us  [the longest x3 7.77 us: take_sequences(): return lax.dynamic_update_slice_in_dim(whole, got, (1 - me) * half, 1)]
    dot_general x130 -> x20, matrix products: 224 us -> 82.2 us  [the longest x12 31.4 us: ein(): return jnp.einsum(form, *operands, preferred_element_type=jnp.float32)]
    another operation x104 -> x2, other arithmetic: 142 us -> 1.89 us
    ppermute x0 -> x13, waiting for transfers between devices: none -> 132 us  [the longest x4 132 us: tp_sum(): other = lax.ppermute(own, 'tp', SWAP)]
    all_gather x8 -> x0, blocking collectives: 127 us -> none  [the longest x1 24.8 us: per_device(): lax.all_gather(w_ssm_bc, ('dp', 'ctx'), axis=0, tiled=True)]
    squeeze x62 -> x0, local copies, waits for them, and re-layouts: 64.7 us -> none  [the longest x40 42.6 us: ssd_one(): lax.scan(jax.checkpoint(block_step), start_state, pieces)]
  transfers between devices with their start and end apart: 28 -> 20, of which waited for: 17 -> 8; matrix products, arithmetic and copies ran while one was open for 43% -> 46% of each run, Pallas kernels for 0% -> 0%
where the time goes in v1:
time: 719 us; the launch traced here: 715 us
  waiting for transfers between devices  267 us (37%)
  matrix products  170 us (24%)
  local copies, waits for them, and re-layouts  122 us (17%)
  other arithmetic  88.2 us (12%)
  blocking collectives  40.9 us (6%)
  between operations  16.8 us (2%)
  starting transfers between devices  8.75 us (1%)
    ppermute x4, waiting for transfers between devices, tp_sum(): other = lax.ppermute(own, 'tp', SWAP)  132 us
    all_gather x2, waiting for transfers between devices, gather_rows(): over_dp = lax.all_gather(shard, 'dp', axis=0, tiled=False)  117 us
    psum x1, blocking collectives, per_device(): small = lax.psum(small, ('dp', 'ctx', 'tp')).reshape(-1)  40.9 us
    dot_general x12, matrix products, ein(): return jnp.einsum(form, *operands, preferred_element_type=jnp.float32)  31.4 us
    dot_general x8, matrix products, dot_left(): lax.dot_general(operand, weight_matrix, (((0,), (0,)), ((), ())), preferr...  29.9 us
    dot_general x4, matrix products, dot_back(): lax.dot_general(operand, weight_matrix, (((1,), (1,)), ((), ())), preferr...  29.1 us
    dot_general x5, matrix products, plain_dot(): return jnp.dot(operand, weight_matrix, preferred_element_type=jnp.float32)  29.1 us
    dot_general x3, matrix products, attend(): jnp.einsum('bcgqk,bkcd->bqcgd', weights, value_rows, preferred_element_ty...  26.2 us
  transfers between devices with their start and end apart: 20, of which 8 were waited for; matrix products, arithmetic and copies ran while one was open for 46% of the time, Pallas kernels for 0%

profile of v1, /device:TPU:0, one launch (start us, length us, event | category | flops | bytes accessed | tf_op | source)
XLA Modules:
  0.0 714.5 jit_solution(6180022355922120818)
XLA Ops:
  15.2 50.4 %all-gather.11.cloned.1.call-done = bf16[512,2304]{1,0:T(8,128)(2,1)} async-done(((bf16[64,2304]{1,0:T(8,128)(2,1)}), bf16[512,2304]{1,0:T(8,128)(2,1)}) %all-gather.11.cloned.1.call-update) | async-done | bytes 2359312 | tf_op jit(solution)/shard_map/all_gather | solution.py:175
  73.5 66.8 %all-gather.13.cloned.1.call-done = bf16[512,4096]{1,0:T(8,128)(2,1)} async-done(((bf16[64,4096]{1,0:T(8,128)(2,1)}), bf16[512,4096]{1,0:T(8,128)(2,1)}) %all-gather.13.cloned.1.call-update) | async-done | bytes 4194320 | tf_op jit(solution)/shard_map/all_gather | solution.py:175
  140.5 14.1 %all-gather.7.cloned.1.call-done = bf16[8,128,2304]{2,1,0:T(8,128)(2,1)} async-done(((bf16[8,64,2304]{2,1,0:T(8,128)(2,1)}), bf16[8,128,2304]{2,1,0:T(8,128)(2,1)}) %all-gather.7.cloned.1.call-update) | async-done | bytes 4718608 | tf_op jit(solution)/shard_map/all_gather | solution.py:176
  154.5 5.8 convolution_convert_fusion.2
  162.5 2.7 copy.112
  169.1 3.1 fusion.11
  172.3 3.7 fusion.259
  178.4 6.4 fusion.105
  189.1 3.7 fusion.70
  192.8 3.5 copy.119
  196.3 5.4 reshape.971
  207.1 4.2 convert_bitcast_fusion.4
  215.7 3.9 copy.122
  219.7 6.7 multiply_convert_fusion.8
  226.4 5.8 convolution_convert_fusion.6
  236.8 3.1 copy.145
  239.8 2.4 constant_dynamic-update-slice_fusion.3
  242.2 38.1 %collective-permute-done.1 = bf16[1024,1024]{1,0:T(8,128)(2,1)} collective-permute-done((bf16[1024,1024]{1,0:T(8,128)(2,1)}, bf16[1024,1024]{1,0:T(8,128)(2,1)}, u32[]{:S(2)}, u32[]{:S(2)}) %collective-permute-start.1) | collective-permute-done | bytes 2097184 | tf_op jit(solution)/shard_map/ppermute | solution.py:169
  280.3 3.2 multiply_reduce_fusion.2
  286.9 4.5 fusion.44
  291.4 7.2 %fusion.31 = (bf16[1024,1024]{1,0:T(8,128)(2,1)S(1)}, bf16[1024,1024]{1,0:T(8,128)(2,1)}, bf16[1024,1024]{1,0:T(8,128)(2,1)}) fusion(f32[1024,2048]{1,0:T(8,128)S(1)} %fusion.44, bf16[1024,4096]{1,0:T(8,128)(2,1)S(1)} %bitcast.709, bf16[1,1024,1024]{2,1,0:T(8,128)(2,1)} %constant_dynamic-update-slice_fusion.3), kind=kOutput, calls=%fused_computation.46 | convolution fusion | flops 2164260864 | bytes 18874368 | tf_op jit(solution)/shard_map/dot_general | solution.py:121
  298.7 8.8 %fusion.273 = (bf16[1024,1024]{1,0:T(8,128)(2,1)S(1)}, f32[1024,1024]{1,0:T(8,128)}) fusion(bf16[1024,4096]{1,0:T(8,128)(2,1)S(1)} %bitcast.710, bf16[1024,1024]{1,0:T(8,128)(2,1)} %get-tuple-element.123, bf16[1024,1024]{1,0:T(8,128)(2,1)S(1)} %get-tuple-element.122), kind=kOutput, calls=%fused_computation.419 | convolution fusion | flops 4304404480 | bytes 14680064 | tf_op jit(solution)/shard_map/dot_general | solution.py:125
  311.0 3.9 copy.148
  321.5 4.0 copy.147
  325.4 3.0 constant_dynamic-slice_fusion.9
  328.4 3.7 convolution_convert_fusion.4
  332.6 3.6 add_convert_fusion.3
  336.3 18.3 %collective-permute-done.5 = bf16[1024,1024]{1,0:T(8,128)(2,1)} collective-permute-done((bf16[1024,1024]{1,0:T(8,128)(2,1)S(1)}, bf16[1024,1024]{1,0:T(8,128)(2,1)}, u32[]{:S(2)}, u32[]{:S(2)}) %collective-permute-start.5) | collective-permute-done | bytes 2097184 | tf_op jit(solution)/shard_map/ppermute | solution.py:169
  354.6 3.7 multiply_reduce_fusion
  358.3 3.5 fusion.260
  361.9 4.8 fusion.76
  371.3 5.4 fusion.63
  378.3 4.0 reshape_reshape.7
  385.7 11.3 %fusion.18 = (f32[4,12,256]{2,1,0:T(8,128)}, f32[4,12,256]{2,1,0:T(8,128)}, f32[4,12,256]{2,1,0:T(8,128)}, bf16[4,256,256]{2,1,0:T(8,128)(2,1)}) fusion(f32[4,12,256]{2,1,0:T(8,128)S(1)} %bitcast.673, f32[4,12,256]{2,1,0:T(8,128)S(1)} %get-tuple-element.193, f32[4,256,256]{2,1,0:T(8,128)} %copy-done.64, pred[256,256]{1,0:T(8,128)(4,1)S(1)} %iota_compare_fusion.1, ...), kind=kOutput, calls=%fused_computation.27 | convolution fusion | flops 449540096 | bytes 6602752 | tf_op jit(solution)/shard_map/transpose(jvp(bkhts,bkhsp->bkhtp))/dot_general | solution.py:69
  398.4 3.2 fusion.55
  403.2 10.6 %fusion.8 = (f32[4,1024]{1,0:T(4,128)}, bf16[4,1024,1024]{1,2,0:T(8,128)(2,1)}) fusion(f32[4,1024]{1,0:T(4,128)} %multiply_divide_fusion, f32[4,1024]{1,0:T(4,128)} %copy-done.123, f32[1024,1024,4]{1,0,2:T(8,128)S(1)} %bitcast.652, pred[1024,1024]{0,1:T(8,128)(4,1)S(1)} %copy-done.39, bf16[64,4,1024]{2,0,1:T(8,128)(2,1)S(1)} %bitcast.683, ...), kind=kOutput, calls=%fused_computation.10 | convolution fusion | flops 570421248 | bytes 27049984 | tf_op jit(solution)/shard_map/transpose(jvp(bcgqk,bkcd->bqcgd))/dot_general | solution.py:59
  414.5 10.3 %fusion.155 = f32[1,1024,1,64]{3,1,2,0:T(8,128)} fusion(bf16[4,1024,1024]{1,2,0:T(8,128)(2,1)} %get-tuple-element.202, f32[4,1024]{1,0:T(4,128)S(1)} %neg.94, f32[4,1024]{1,0:T(4,128)S(1)} %copy-done.105, pred[1024,1024]{0,1:T(8,128)(4,1)S(1)} %copy-done.39, bf16[1024,4,32]{0,2,1:T(8,128)(2,1)S(1)} %copy-done.84, bf16[1024,4,32]{0,2,1:T(8,128)(2,1)S(1)} %copy-done.82, ...), kind=kOutput, calls=%fused_computation.195 | convolution fusion | flops 575799296 | bytes 27049984 | tf_op jit(solution)/shard_map/transpose(jvp(bqcgd,bkcd->bcgqk))/dot_general | solution.py:52
  424.9 10.6 %fusion.123 = f32[1,1024,4,64]{1,3,2,0:T(8,128)} fusion(bf16[4,1024,1024]{1,2,0:T(8,128)(2,1)} %get-tuple-element.202, f32[4,1024]{1,0:T(4,128)S(1)} %neg.94, f32[4,1024]{1,0:T(4,128)S(1)} %copy-done.105, pred[1024,1024]{0,1:T(8,128)(4,1)S(1)} %copy-done.40, bf16[1024,32]{1,0:T(8,128)(2,1)S(1)} %copy-done.88, bf16[1024,32]{1,0:T(8,128)(2,1)S(1)} %copy-done.86, ...), kind=kOutput, calls=%fused_computation.181 | convolution fusion | flops 575406080 | bytes 27443200 | tf_op jit(solution)/shard_map/transpose(jvp(bqcgd,bkcd->bcgqk))/dot_general | solution.py:52
  435.6 2.7 copy.146
  446.7 2.9 multiply_add_fusion.3
  451.6 5.2 fusion.47
  456.8 5.3 add_convert_fusion.1
  463.2 3.9 copy.130
  467.1 3.1 reshape.979
  470.1 3.9 copy.131
  474.1 3.9 pad_maximum_fusion.1
  480.1 3.5 add_convert_fusion.4
  483.7 3.5 broadcast_multiply_fusion.4
  487.2 4.4 multiply_reduce_fusion.6
  491.7 3.9 broadcast_multiply_fusion
  499.0 3.3 fusion.172
  502.3 4.1 fusion.84
  506.5 9.2 %fusion.142 = bf16[1024,64]{1,0:T(8,128)(2,1)} fusion(bf16[64,4,1024]{2,0,1:T(8,128)(2,1)S(1)} %bitcast.684, f32[4,1024]{1,0:T(4,128)S(1)} %copy-done.105, f32[4,1024]{1,0:T(4,128)S(1)} %copy-done.124, f32[1024,1024,4]{1,0,2:T(8,128)} %copy-done.13, pred[1024,1024]{0,1:T(8,128)(4,1)S(1)} %copy-done.41), kind=kOutput, calls=%fused_computation.190 | convolution fusion | flops 557907968 | bytes 18513920 | tf_op jit(solution)/shard_map/transpose(jvp(bcgqk,bkcd->bqcgd))/dot_general | solution.py:59
  515.8 7.0 concatenate.64
  522.8 5.4 convolution_convert_fusion.1
  528.8 9.3 %fusion.274 = (bf16[1024,1024]{1,0:T(8,128)(2,1)}, f32[1024,1024]{1,0:T(8,128)}) fusion(bf16[1024,2304]{1,0:T(8,128)(2,1)S(1)} %copy-done.36, bf16[1024,2304]{1,0:T(8,128)(2,1)} %bitcast.713), kind=kOutput, calls=%fused_computation.420 | convolution fusion | flops 4832886784 | bytes 15728640 | tf_op jit(solution)/shard_map/dot_general | solution.py:125
  539.8 5.3 convolution_convert_fusion.5
  545.4 3.9 add_convert_fusion
  549.5 37.4 %collective-permute-done.6 = bf16[1024,1024]{1,0:T(8,128)(2,1)} collective-permute-done((bf16[1024,1024]{1,0:T(8,128)(2,1)}, bf16[1024,1024]{1,0:T(8,128)(2,1)}, u32[]{:S(2)}, u32[]{:S(2)}) %collective-permute-start.6) | collective-permute-done | bytes 2097184 | tf_op jit(solution)/shard_map/ppermute | solution.py:169
  587.0 5.4 fusion.38
  592.4 38.6 %collective-permute-done.2 = bf16[1024,1024]{1,0:T(8,128)(2,1)} collective-permute-done((bf16[1024,1024]{1,0:T(8,128)(2,1)}, bf16[1024,1024]{1,0:T(8,128)(2,1)}, u32[]{:S(2)}, u32[]{:S(2)}) %collective-permute-start.2) | collective-permute-done | bytes 2097184 | tf_op jit(solution)/shard_map/ppermute | solution.py:169
  631.1 7.1 fusion.34
  641.4 40.9 %psum.7 = f32[80,128]{1,0:T(8,128)S(1)} all-reduce(f32[80,128]{1,0:T(8,128)S(1)} %fusion.229), channel_id=1, replica_groups=mesh['dp'=8,'ctx'=2,'tp'=2] {'dp','ctx','tp'}, use_global_device_ids=true, to_apply=%region_30.31 | all-reduce | flops 10240 | bytes 81920 | tf_op jit(solution)/shard_map/psum | solution.py:376
  694.7 3.3 reduce-scatter.4.cloned.1.call-done
  (492 shorter events, 113.9 us)
Async XLA Ops:
  7.2 58.4 %all-gather.11.cloned.1.call-start = ((), (), s32[]{:S(2)}) async-start(), calls=%async_computation.8 | async-start | bytes 2654208 | tf_op jit(solution)/shard_map/all_gather | solution.py:175
  9.9 130.4 %all-gather.13.cloned.1.call-start = ((), (), s32[]{:S(2)}) async-start(), calls=%async_computation.9 | async-start | bytes 4718592 | tf_op jit(solution)/shard_map/all_gather | solution.py:175
  15.2 139.4 %all-gather.7.cloned.1.call-start = ((), (), s32[]{:S(2)}) async-start(), calls=%async_computation.3 | async-start | bytes 7077888 | tf_op jit(solution)/shard_map/all_gather | solution.py:176
  65.6 160.8 %all-gather.9.cloned.1.call-start = ((), (), s32[]{:S(2)}) async-start(), calls=%async_computation.4 | async-start | bytes 12582912 | tf_op jit(solution)/shard_map/all_gather | solution.py:176
  67.7 3.8 collective-permute-start
  68.9 96.3 %copy-start.134 = (f32[32]{0:T(128)}, f32[32]{0:T(128)S(1)}, u32[]{:S(2)}) copy-start(f32[32]{0:T(128)S(1)} %multiply_power_fusion) | copy-start | bytes 388
  68.9 316.7 %copy-start.101 = (pred[256,256]{1,0:T(8,128)(4,1)}, pred[256,256]{1,0:T(8,128)(4,1)S(1)}, u32[]{:S(2)}) copy-start(pred[256,256]{1,0:T(8,128)(4,1)S(1)} %iota_compare_fusion.1) | copy-start | bytes 196612
  69.0 120.1 %copy-start.114 = (f32[768]{0:T(1024)}, f32[768]{0:T(1024)S(1)}, u32[]{:S(2)}) copy-start(f32[768]{0:T(1024)S(1)} %get-tuple-element.106) | copy-start | bytes 9220
  69.0 120.1 %copy-start.116 = (f32[768]{0:T(1024)}, f32[768]{0:T(1024)S(1)}, u32[]{:S(2)}) copy-start(f32[768]{0:T(1024)S(1)} %get-tuple-element.107) | copy-start | bytes 9220
  69.0 120.1 %copy-start.118 = (f32[768]{0:T(1024)}, f32[768]{0:T(1024)S(1)}, u32[]{:S(2)}) copy-start(f32[768]{0:T(1024)S(1)} %get-tuple-element.108) | copy-start | bytes 9220
  69.0 120.1 %copy-start.120 = (f32[768]{0:T(1024)}, f32[768]{0:T(1024)S(1)}, u32[]{:S(2)}) copy-start(f32[768]{0:T(1024)S(1)} %get-tuple-element.109) | copy-start | bytes 9220
  70.9 131.5 %copy-start.126 = (f32[1,256]{1,0:T(1,128)}, f32[1,256]{1,0:T(1,128)S(1)}, u32[]{:S(2)}) copy-start(f32[1,256]{1,0:T(1,128)S(1)} %get-tuple-element.180) | copy-start | bytes 3076
  70.9 131.5 %copy-start.128 = (f32[1,256]{1,0:T(1,128)}, f32[1,256]{1,0:T(1,128)S(1)}, u32[]{:S(2)}) copy-start(f32[1,256]{1,0:T(1,128)S(1)} %get-tuple-element.181) | copy-start | bytes 3076
  71.5 95.9 %copy-start.55 = (f32[1024,32]{0,1:T(8,128)}, f32[1024,32]{0,1:T(8,128)S(1)}, u32[]{:S(2)}) copy-start(f32[1024,32]{0,1:T(8,128)S(1)} %get-tuple-element.190) | copy-start | bytes 393220
  71.5 95.9 %copy-start.57 = (f32[1024,32]{0,1:T(8,128)}, f32[1024,32]{0,1:T(8,128)S(1)}, u32[]{:S(2)}) copy-start(f32[1024,32]{0,1:T(8,128)S(1)} %get-tuple-element.191) | copy-start | bytes 393220
  72.9 207.4 %copy-start.7 = (bf16[1,1024,1024]{2,1,0:T(8,128)(2,1)}, bf16[1,1024,1024]{2,1,0:T(8,128)(2,1)S(1)}, u32[]{:S(2)}) copy-start(bf16[1,1024,1024]{2,1,0:T(8,128)(2,1)S(1)} %constant_dynamic-update-slice_fusion.5) | copy-start | bytes 6291460
  72.9 81.6 %copy-start.108 = (f32[1024]{0:T(1024)S(1)}, f32[1024]{0:T(1024)}, u32[]{:S(2)}) copy-start(f32[1024]{0:T(1024)} %param.23) | copy-start | bytes 12292
  73.4 86.9 %copy-start.112 = (f32[1024]{0:T(1024)}, f32[1024]{0:T(1024)S(1)}, u32[]{:S(2)}) copy-start(f32[1024]{0:T(1024)S(1)} %fusion.39) | copy-start | bytes 12292
  73.5 235.8 %copy-start.94 = (f32[1024]{0:T(1024)}, f32[1024]{0:T(1024)S(1)}, u32[]{:S(2)}) copy-start(f32[1024]{0:T(1024)S(1)} %fusion.233) | copy-start | bytes 12292
  140.3 546.8 %reduce-scatter.6.cloned.1.call-start = ((), (), s32[]{:S(2)}) async-start(), calls=%async_computation.6 | async-start | bytes 1179648 | tf_op jit(solution)/shard_map/reduce_scatter | solution.py:195
  178.4 142.5 %copy-start.104 = (f32[4,1024]{1,0:T(4,128)}, f32[4,1024]{1,0:T(4,128)S(1)}, u32[]{:S(2)}) copy-start(f32[4,1024]{1,0:T(4,128)S(1)} %fusion.259) | copy-start | bytes 49156
  187.2 198.4 %copy-start.52 = (f32[1,4,256,12]{2,3,1,0:T(8,128)}, f32[1,4,256,12]{2,3,1,0:T(8,128)S(1)}, u32[]{:S(2)}) copy-start(f32[1,4,256,12]{2,3,1,0:T(8,128)S(1)} %copy.118) | copy-start | bytes 147460
  202.0 180.3 %copy-start.96 = (f32[4,12,256]{2,1,0:T(8,128)}, f32[4,12,256]{2,1,0:T(8,128)S(1)}, u32[]{:S(2)}) copy-start(f32[4,12,256]{2,1,0:T(8,128)S(1)} %get-tuple-element.192) | copy-start | bytes 147460
  202.0 183.6 %copy-start.50 = (f32[4,12,256]{2,1,0:T(8,128)}, f32[4,12,256]{2,1,0:T(8,128)S(1)}, u32[]{:S(2)}) copy-start(f32[4,12,256]{2,1,0:T(8,128)S(1)} %get-tuple-element.193) | copy-start | bytes 147460
  232.2 48.1 %collective-permute-start.1 = (bf16[1024,1024]{1,0:T(8,128)(2,1)}, bf16[1024,1024]{1,0:T(8,128)(2,1)}, u32[]{:S(2)}, u32[]{:S(2)}) collective-permute-start(bf16[1024,1024]{1,0:T(8,128)(2,1)} %convolution_convert_fusion.6), channel_id=1, source_target_pairs={{0,1},{1,0},{2,3},{3,2},{4,5},{5,4},{6,7},{7,6},{8,9},{9,8},{10,11... | collective-permute-start | bytes 6291464 | tf_op jit(solution)/shard_map/ppermute | solution.py:169
  236.7 3.1 collective-permute-start.4
  239.8 47.1 %slice-start.4 = ((s8[8388608]{0:T(1024)(128)(4,1)}), s8[4194304]{0:T(1024)(128)(4,1)S(1)}, s32[]{:S(2)}) async-start(s8[8388608]{0:T(1024)(128)(4,1)} %bitcast.706), calls=%async_computation.14 | async-start | bytes 8388608
  242.2 41.3 %copy-start.92 = (f32[1024]{0:T(1024)S(1)}, f32[1024]{0:T(1024)}, u32[]{:S(2)}) copy-start(f32[1024]{0:T(1024)} %param.24) | copy-start | bytes 12292
  242.2 44.7 %slice-start.5 = ((s8[8388608]{0:T(1024)(128)(4,1)}), s8[4194304]{0:T(1024)(128)(4,1)S(1)}, s32[]{:S(2)}) async-start(s8[8388608]{0:T(1024)(128)(4,1)} %bitcast.706), calls=%async_computation.15 | async-start | bytes 8388608
  283.6 74.7 %copy-start.90 = (f32[1024]{0:T(1024)}, f32[1024]{0:T(1024)S(1)}, u32[]{:S(2)}) copy-start(f32[1024]{0:T(1024)S(1)} %fusion.234) | copy-start | bytes 12292
  307.5 50.8 %copy-start.11 = (bf16[1024,1024]{1,0:T(8,128)(2,1)}, bf16[1024,1024]{1,0:T(8,128)(2,1)S(1)}, u32[]{:S(2)}) copy-start(bf16[1024,1024]{1,0:T(8,128)(2,1)S(1)} %get-tuple-element.198) | copy-start | bytes 6291460
  307.5 47.1 %collective-permute-start.5 = (bf16[1024,1024]{1,0:T(8,128)(2,1)S(1)}, bf16[1024,1024]{1,0:T(8,128)(2,1)}, u32[]{:S(2)}, u32[]{:S(2)}) collective-permute-start(bf16[1024,1024]{1,0:T(8,128)(2,1)S(1)} %get-tuple-element.198), channel_id=1, source_target_pairs={{0,1},{1,0},{2,3},{3,2},{4,5},{5,4},{6,7},{7,6},{8,9},{9,8},{10,11... | collective-permute-start | bytes 6291464 | tf_op jit(solution)/shard_map/ppermute | solution.py:169
  319.4 13.2 %collective-permute-start.12 = (bf16[512,1024]{1,0:T(8,128)(2,1)}, bf16[512,1024]{1,0:T(8,128)(2,1)}, u32[]{:S(2)}, u32[]{:S(2)}) collective-permute-start(bf16[512,1024]{1,0:T(8,128)(2,1)} %convolution_convert_fusion.8), channel_id=1, source_target_pairs={{0,2},{2,0},{1,3},{3,1},{4,6},{6,4},{5,7},{7,5},{8,10},{10,8},{9,1... | collective-permute-start | bytes 3145736 | tf_op jit(solution)/shard_map/ppermute | solution.py:190
  332.1 124.6 %collective-permute-start.11 = (bf16[512,2048]{1,0:T(8,128)(2,1)}, bf16[512,2048]{1,0:T(8,128)(2,1)}, u32[]{:S(2)}, u32[]{:S(2)}) collective-permute-start(bf16[512,2048]{1,0:T(8,128)(2,1)} %convolution_convert_fusion.4), channel_id=1, source_target_pairs={{0,2},{2,0},{1,3},{3,1},{4,6},{6,4},{5,7},{7,5},{8,10},{10,8},{9,1... | collective-permute-start | bytes 6291464 | tf_op jit(solution)/shard_map/ppermute | solution.py:190
  332.6 22.0 %copy-start.3 = (f32[1024,1024]{1,0:T(8,128)S(1)}, f32[1024,1024]{1,0:T(8,128)}, u32[]{:S(2)}) copy-start(f32[1024,1024]{1,0:T(8,128)} %copy-done.2) | copy-start | bytes 12582916
  332.6 22.0 %copy-start.42 = (f32[1024,1024]{1,0:T(8,128)S(1)}, f32[1024,1024]{1,0:T(8,128)}, u32[]{:S(2)}) copy-start(f32[1024,1024]{1,0:T(8,128)} %get-tuple-element.199) | copy-start | bytes 12582916
  382.3 20.8 %slice-start = ((s8[16777216]{0:T(1024)(128)(4,1)}), s8[4194304]{0:T(1024)(128)(4,1)S(1)}, s32[]{:S(2)}) async-start(s8[16777216]{0:T(1024)(128)(4,1)} %bitcast.651), calls=%async_computation.10 | async-start | bytes 8388608
  385.6 12.7 %copy-start.18 = (f32[4,12,64,256]{3,2,1,0:T(8,128)S(1)}, f32[4,12,64,256]{3,2,1,0:T(8,128)}, u32[]{:S(2)}) copy-start(f32[4,12,64,256]{3,2,1,0:T(8,128)} %copy-done.17) | copy-start | bytes 9437188
  385.7 12.7 %copy-start.34 = (bf16[1,4,256,12,64]{2,1,4,3,0:T(4,128)(2,1)S(1)}, bf16[1,4,256,12,64]{2,1,4,3,0:T(4,128)(2,1)}, u32[]{:S(2)}) copy-start(bf16[1,4,256,12,64]{2,1,4,3,0:T(4,128)(2,1)} %reshape_reshape.7) | copy-start | bytes 4718596
  385.7 17.5 %slice-start.1 = ((s8[16777216]{0:T(1024)(128)(4,1)}), s8[4194304]{0:T(1024)(128)(4,1)S(1)}, s32[]{:S(2)}) async-start(s8[16777216]{0:T(1024)(128)(4,1)} %bitcast.651), calls=%async_computation.11 | async-start | bytes 8388608
  385.7 17.4 %slice-start.2 = ((s8[16777216]{0:T(1024)(128)(4,1)}), s8[4194304]{0:T(1024)(128)(4,1)S(1)}, s32[]{:S(2)}) async-start(s8[16777216]{0:T(1024)(128)(4,1)} %bitcast.651), calls=%async_computation.12 | async-start | bytes 8388608
  385.7 17.4 %slice-start.3 = ((s8[16777216]{0:T(1024)(128)(4,1)}), s8[4194304]{0:T(1024)(128)(4,1)S(1)}, s32[]{:S(2)}) async-start(s8[16777216]{0:T(1024)(128)(4,1)} %bitcast.651), calls=%async_computation.13 | async-start | bytes 8388608
  403.2 11.3 %copy-start.82 = (bf16[1024,4,32]{0,2,1:T(8,128)(2,1)S(1)}, bf16[1024,4,32]{0,2,1:T(8,128)(2,1)}, u32[]{:S(2)}) copy-start(bf16[1024,4,32]{0,2,1:T(8,128)(2,1)} %copy-done.81) | copy-start | bytes 786436
  403.2 11.3 %copy-start.84 = (bf16[1024,4,32]{0,2,1:T(8,128)(2,1)S(1)}, bf16[1024,4,32]{0,2,1:T(8,128)(2,1)}, u32[]{:S(2)}) copy-start(bf16[1024,4,32]{0,2,1:T(8,128)(2,1)} %copy-done.83) | copy-start | bytes 786436
  446.2 33.7 %collective-permute-start.9 = (bf16[512,1024]{1,0:T(8,128)(2,1)}, bf16[512,1024]{1,0:T(8,128)(2,1)}, u32[]{:S(2)}, u32[]{:S(2)}) collective-permute-start(bf16[512,1024]{1,0:T(8,128)(2,1)} %convolution_convert_fusion.9), channel_id=1, source_target_pairs={{0,2},{2,0},{1,3},{3,1},{4,6},{6,4},{5,7},{7,5},{8,10},{10,8},{9,1... | collective-permute-start | bytes 3145736 | tf_op jit(solution)/shard_map/ppermute | solution.py:190
  483.6 208.2 %reduce-scatter.8.cloned.1.call-start = ((), (), s32[]{:S(2)}) async-start(), calls=%async_computation.7 | async-start | bytes 3538944 | tf_op jit(solution)/shard_map/reduce_scatter | solution.py:195
  495.6 202.5 %reduce-scatter.4.cloned.1.call-start = ((), (), s32[]{:S(2)}) async-start(), calls=%async_computation.5 | async-start | bytes 2654208 | tf_op jit(solution)/shard_map/reduce_scatter | solution.py:195
  528.2 11.6 %copy-start.151 = (bf16[1024,1024]{1,0:T(8,128)(2,1)S(1)}, bf16[1024,1024]{1,0:T(8,128)(2,1)}, u32[]{:S(2)}) copy-start(bf16[1024,1024]{1,0:T(8,128)(2,1)} %get-tuple-element.124) | copy-start | bytes 6291460
  528.2 17.2 %collective-permute-start.8 = (bf16[512,2304]{1,0:T(8,128)(2,1)S(1)}, bf16[512,2304]{1,0:T(8,128)(2,1)S(1)}, u32[]{:S(2)}, u32[]{:S(2)}) collective-permute-start(bf16[512,2304]{1,0:T(8,128)(2,1)S(1)} %convolution_convert_fusion.1), channel_id=1, source_target_pairs={{0,2},{2,0},{1,3},{3,1},{4,6},{6,4},{5,7},{7,5},{8,10},{10,8},{9,1... | collective-permute-start | bytes 7077896 | tf_op jit(solution)/shard_map/ppermute | solution.py:190
  538.1 48.8 %collective-permute-start.6 = (bf16[1024,1024]{1,0:T(8,128)(2,1)}, bf16[1024,1024]{1,0:T(8,128)(2,1)}, u32[]{:S(2)}, u32[]{:S(2)}) collective-permute-start(bf16[1024,1024]{1,0:T(8,128)(2,1)} %get-tuple-element.203), channel_id=1, source_target_pairs={{0,1},{1,0},{2,3},{3,2},{4,5},{5,4},{6,7},{7,6},{8,9},{9,8},{10,11... | collective-permute-start | bytes 6291464 | tf_op jit(solution)/shard_map/ppermute | solution.py:169
  545.1 86.0 %collective-permute-start.2 = (bf16[1024,1024]{1,0:T(8,128)(2,1)}, bf16[1024,1024]{1,0:T(8,128)(2,1)}, u32[]{:S(2)}, u32[]{:S(2)}) collective-permute-start(bf16[1024,1024]{1,0:T(8,128)(2,1)} %convolution_convert_fusion.5), channel_id=1, source_target_pairs={{0,1},{1,0},{2,3},{3,2},{4,5},{5,4},{6,7},{7,6},{8,9},{9,8},{10,11... | collective-permute-start | bytes 6291464 | tf_op jit(solution)/shard_map/ppermute | solution.py:169
  545.4 41.5 %copy-start.95 = (f32[1024]{0:T(1024)S(1)}, f32[1024]{0:T(1024)}, u32[]{:S(2)}) copy-start(f32[1024]{0:T(1024)} %copy-done.94) | copy-start | bytes 12292
  545.4 41.5 %copy-start.109 = (f32[1024]{0:T(1024)S(1)}, f32[1024]{0:T(1024)}, u32[]{:S(2)}) copy-start(f32[1024]{0:T(1024)} %param.23) | copy-start | bytes 12292
  549.3 37.6 %copy-start.8 = (bf16[1,1024,1024]{2,1,0:T(8,128)(2,1)S(1)}, bf16[1,1024,1024]{2,1,0:T(8,128)(2,1)}, u32[]{:S(2)}) copy-start(bf16[1,1024,1024]{2,1,0:T(8,128)(2,1)} %copy-done.7) | copy-start | bytes 6291460
  586.9 44.1 %copy-start.4 = (f32[1024,1024]{1,0:T(8,128)S(1)}, f32[1024,1024]{1,0:T(8,128)}, u32[]{:S(2)}) copy-start(f32[1024,1024]{1,0:T(8,128)} %copy-done.2) | copy-start | bytes 12582916
  587.0 44.1 %copy-start.12 = (bf16[1024,1024]{1,0:T(8,128)(2,1)S(1)}, bf16[1024,1024]{1,0:T(8,128)(2,1)}, u32[]{:S(2)}) copy-start(bf16[1024,1024]{1,0:T(8,128)(2,1)} %copy-done.11) | copy-start | bytes 6291460
  587.0 44.1 %copy-start.91 = (f32[1024]{0:T(1024)S(1)}, f32[1024]{0:T(1024)}, u32[]{:S(2)}) copy-start(f32[1024]{0:T(1024)} %copy-done.90) | copy-start | bytes 12292
  587.0 44.1 %copy-start.93 = (f32[1024]{0:T(1024)S(1)}, f32[1024]{0:T(1024)}, u32[]{:S(2)}) copy-start(f32[1024]{0:T(1024)} %param.24) | copy-start | bytes 12292
  587.0 44.1 %copy-start.111 = (f32[1024]{0:T(1024)S(1)}, f32[1024]{0:T(1024)}, u32[]{:S(2)}) copy-start(f32[1024]{0:T(1024)} %copy-done.110) | copy-start | bytes 12292
  639.3 48.7 %collective-permute-start.7 = (bf16[1,512,1024]{2,1,0:T(8,128)(2,1)}, bf16[1,512,1024]{2,1,0:T(8,128)(2,1)}, u32[]{:S(2)}, u32[]{:S(2)}) collective-permute-start(bf16[1,512,1024]{2,1,0:T(8,128)(2,1)} %dynamic-slice_bitcast_fusion), channel_id=1, source_target_pairs={{0,2},{2,0},{1,3},{3,1},{4,6},{6,4},{5,7},{7,5},{8,10},{10,8},{9,1... | collective-permute-start | bytes 3145736 | tf_op jit(solution)/shard_map/ppermute | solution.py:161
  640.9 49.4 %collective-permute-start.3 = (bf16[1,512,1024]{2,1,0:T(8,128)(2,1)}, bf16[1,512,1024]{2,1,0:T(8,128)(2,1)S(1)}, u32[]{:S(2)}, u32[]{:S(2)}) collective-permute-start(bf16[1,512,1024]{2,1,0:T(8,128)(2,1)} %dynamic-slice_bitcast_fusion.1), channel_id=1, source_target_pairs={{0,2},{2,0},{1,3},{3,1},{4,6},{6,4},{5,7},{7,5},{8,10},{10,8},{9,1... | collective-permute-start | bytes 3145736 | tf_op jit(solution)/shard_map/ppermute | solution.py:161
  640.9 44.2 %copy-start.24 = (bf16[1024,1024]{1,0:T(8,128)(2,1)S(1)}, bf16[1024,1024]{1,0:T(8,128)(2,1)}, u32[]{:S(2)}) copy-start(bf16[1024,1024]{1,0:T(8,128)(2,1)} %copy-done.23) | copy-start | bytes 6291460
  690.4 16.8 %copy-start.47 = (bf16[2,512,1024]{2,1,0:T(8,128)(2,1)}, bf16[2,512,1024]{2,1,0:T(8,128)(2,1)S(1)}, u32[]{:S(2)}) copy-start(bf16[2,512,1024]{2,1,0:T(8,128)(2,1)S(1)} %constant_dynamic-update-slice_fusion.4) | copy-start | bytes 6291460
  699.5 7.1 collective-permute-start.10
  (121 other events, 481.2 us)
Sparse Core Ops, SparseCore 0:
  10.8 54.7 all-gather.10
  68.3 71.9 all-gather.12
  141.8 12.6 all-gather.6
  155.9 21.0 all-gather.8
  483.7 64.7 reduce-scatter.5
  552.4 73.4 reduce-scatter.7
  629.8 68.2 reduce-scatter.3
